TPU v7x, 32 devices: a whole 2x2x4 slice. The times are simulated.
32 devices in a mesh: groups: 2 (over x), date: 16 (over z, y, core).
Axes of the slice: x: 2, y: 2, z: 4, core: 2. Of those that a mesh axis runs over, the one named last changes fastest.
Arguments:
- images: float32 [32, 2, 64, 2560], P(('groups', 'date')), parts along dimension 0, may hold values from -16 to 16
- height_phase: float32 [128, 2560], P(('groups', 'date')), parts along dimension 0, may hold values from -4 to 4
- baseline: float32 [32], P('groups'), parts along dimension 0, may hold values from -0.6 to 0.6
- pair_list: int32 [32, 2], replicated, may hold values from 0 to 15, as said below
- pair_owner: int32 [32, 1], replicated, may hold values from 0 to 15; in each aligned block of 32 rows (0 to 31, 32 to 63, ...) at most 4 rows name the same one
Outputs:
- interferogram: float32 [128, 2, 16, 128], P(('groups', 'date')), parts along dimension 0
- coherence: float32 [128, 16, 128], P(('groups', 'date')), parts along dimension 0
There are 2 independent parts, one for each index of `groups`. A program takes and returns all parts, laid end to end along the dimension named above; an argument that names none is the same for every part. Nothing has to cross between parts.
Inputs may be any that keep to these rules, and one draw needn't show every extreme that they name: `pair_list`: each row is (r, s) with r < s <= r + 4; some pair has s = r + 4. `pair_owner`: every index owns at least one pair and at most 4 pairs; some index owns exactly 4.
All inputs are finite; a program needn't handle non-finite values.
Results may differ from a plain program's by a relative error of at most 0.00007.
Values sent between devices are 32-bit elements; how exact they have to be, the bound alone decides.
No kernel may reach another device: no remote copies, remote signals or barrier semaphores. Data moves between devices by JAX's collectives and lax.ppermute only.
A program may use at most 128 MiB of HBM per device.

v0:
```python
import jax
import jax.numpy as jnp
from jax import lax
from jax.sharding import PartitionSpec as P

LOOK_ROWS = 4
LOOK_COLS = 20
CAP = 4


EPSILON = 1e-06


def box_matrix(columns):
    position = jnp.arange(columns, dtype=jnp.int32)
    target = jnp.arange(columns // LOOK_COLS, dtype=jnp.int32)
    return (position[:, None] // LOOK_COLS == target[None, :]).astype(jnp.float32)


def multilook(values):
    values_shape = values.shape
    row_count = values_shape[-2]
    columns = values_shape[-1]
    summed = jnp.sum(
        values.reshape(values_shape[:-2] + (row_count // LOOK_ROWS, LOOK_ROWS, columns)), axis=-2
    )
    flattened = summed.reshape(-1, columns)
    looked = jnp.dot(
        flattened,
        box_matrix(columns),
        precision=lax.Precision.HIGHEST,
        preferred_element_type=jnp.float32,
    )
    return looked.reshape(values_shape[:-2] + (row_count // LOOK_ROWS, columns // LOOK_COLS)) / (
        LOOK_ROWS * LOOK_COLS
    )


def flatten_phase(images, factors, height_phase):
    phase_angle = factors[:, None, None] * height_phase[None]
    cosine = jnp.cos(phase_angle)
    sine_part = jnp.sin(phase_angle)
    real_part = images[:, 0] * cosine - images[:, 1] * sine_part
    imag_part = images[:, 0] * sine_part + images[:, 1] * cosine
    return (real_part, imag_part)


def pair_terms(first_real, first_imag, second_real, second_imag, first_power, second_power):
    look_real = multilook(first_real * second_real + first_imag * second_imag)
    look_imag = multilook(first_imag * second_real - first_real * second_imag)
    denominator = jnp.sqrt((first_power + EPSILON) * (second_power + EPSILON))
    coherence = jnp.sqrt(look_real * look_real + look_imag * look_imag) / denominator
    return jnp.stack([look_real, look_imag, coherence], axis=-3)


def body(images, height_phase, baseline, pair_list, pair_owner):
    devices = lax.axis_size("date")
    owners = pair_owner[:, 0]
    first_index = pair_list[:, 0]
    second_index = pair_list[:, 1]
    gathered = lax.all_to_all(images, "date", split_axis=2, concat_axis=0, tiled=True)
    real_part, imag_part = flatten_phase(gathered, baseline, height_phase)
    power_map = multilook(real_part * real_part + imag_part * imag_part)
    quantities = pair_terms(
        real_part[first_index],
        imag_part[first_index],
        real_part[second_index],
        imag_part[second_index],
        power_map[first_index],
        power_map[second_index],
    )
    source = jnp.arange(pair_list.shape[0], dtype=jnp.int32)
    position = jnp.arange(owners.shape[0], dtype=jnp.int32)
    earlier = (owners[:, None] == owners[None, :]) & (position[:, None] > position[None, :])
    slot_index = owners * CAP + jnp.sum(earlier.astype(jnp.int32), axis=1)
    slot_count = CAP * devices
    slot_range = jnp.arange(slot_count, dtype=jnp.int32)
    taken = (slot_index[None, :] == slot_range[:, None]).astype(jnp.int32)
    picked = jnp.sum(taken * (source[None, :] + 1), axis=1) - 1
    column_range = jnp.arange(quantities.shape[0], dtype=jnp.int32)
    selector = (picked[:, None] == column_range[None, :]).astype(jnp.float32)
    buffer = jnp.einsum(
        "sq,qkrc->skrc",
        selector,
        quantities,
        precision=lax.Precision.HIGHEST,
        preferred_element_type=jnp.float32,
    )
    delivered = lax.all_to_all(buffer, "date", split_axis=0, concat_axis=2, tiled=True)
    return (delivered[:, :2], delivered[:, 2])


def solution(mesh):
    in_specs = (
        P(("groups", "date"), None, None, None),
        P(("groups", "date"), None),
        P("groups"),
        P(),
        P(),
    )
    out_specs = (P(("groups", "date"), None, None, None), P(("groups", "date"), None, None))
    return jax.shard_map(body, mesh=mesh, in_specs=in_specs, out_specs=out_specs, check_vma=False)
```

profile of v0, /device:TPU:0, one launch (start us, length us, event | category | flops | bytes accessed | tf_op | source)
XLA Modules:
  0.0 79.1 jit_solution(1218121472605938797)
XLA Ops:
  0.6 3.4 %copy.25 = f32[1,2,64,2560]{3,1,0,2:T(2,128)} copy(f32[1,2,64,2560]{3,2,1,0:T(8,128)} %param.5) | data formatting | bytes 2621440 | tf_op args[0]
  4.0 0.0 copy-start.2
  4.0 0.0 copy-start.3
  4.0 7.5 %all-to-all-start = ((f32[1,2,64,2560]{3,1,0,2:T(2,128)}), f32[1,2,64,2560]{3,1,0,2:T(2,128)S(1)}, u32[]{:S(2)}, u32[]{:S(2)}) async-start(f32[1,2,64,2560]{3,1,0,2:T(2,128)} %copy.25), calls=%async_computation | async-start | bytes 2621440 | tf_op jit(solution)/shard_map/all_to_all | solution.py:61
  11.5 0.0 copy-done.2
  11.6 0.0 copy-done.3
  11.6 0.2 convert_reduce_fusion
  11.8 0.1 select_reduce_fusion
  11.9 27.1 %all-to-all-done = f32[1,2,64,2560]{3,1,0,2:T(2,128)S(1)} async-done(((f32[1,2,64,2560]{3,1,0,2:T(2,128)}), f32[1,2,64,2560]{3,1,0,2:T(2,128)S(1)}, u32[]{:S(2)}, u32[]{:S(2)}) %all-to-all-start) | async-done | bytes 1310752 | tf_op jit(solution)/shard_map/all_to_all | solution.py:61
  39.0 0.0 copy-start
  39.0 0.0 copy-start.1
  39.0 0.8 copy.36
  39.7 0.0 copy-done
  39.7 0.0 copy-done.1
  39.8 2.9 %fusion.17 = f32[16,2560]{1,0:T(8,128)S(1)} fusion(f32[16,2,4,2560]{3,0,2,1:T(8,128)S(1)} %bitcast.41, f32[4,2560]{1,0:T(4,128)S(1)} %copy-done, f32[16]{0:T(128)S(1)} %copy-done.1), kind=kLoop, calls=%fused_computation.32 | loop fusion | flops 1761280 | bytes 1515584 | tf_op jit(solution)/shard_map/reduce_sum | solution.py:24
  42.6 3.4 %fusion.20 = (f32[16,4,2560]{2,0,1:T(8,128)}, f32[16,4,2560]{2,0,1:T(8,128)S(1)}) fusion(f32[16,2,4,2560]{3,0,2,1:T(8,128)S(1)} %bitcast.42, f32[4,2560]{1,0:T(4,128)S(1)} %copy-done, f32[16]{0:T(128)S(1)} %copy-done.1), kind=kLoop, calls=%fused_computation.35 | loop fusion | flops 1146880 | bytes 2662464 | tf_op jit(solution)/shard_map/sub | solution.py:43
  46.0 0.7 fusion.5
  46.7 0.6 gather_fusion.5
  47.3 0.6 gather_fusion.4
  47.9 0.4 copy.29
  48.3 1.3 %gather_fusion.2 = f32[32,4,2560]{2,1,0:T(4,128)S(1)} fusion(f32[16,4,2560]{2,1,0:T(4,128)S(1)} %copy.29, s32[1024]{0:T(1024)S(1)} %get-tuple-element.21), kind=kCustom, calls=%fused_computation.2 | custom fusion | bytes 2621568 | tf_op jit(solution)/shard_map/gather | solution.py:66
  49.7 1.3 %gather_fusion.3 = f32[32,4,2560]{2,1,0:T(4,128)S(1)} fusion(f32[16,4,2560]{2,1,0:T(4,128)S(1)} %copy.29, s32[1024]{0:T(1024)S(1)} %get-tuple-element.20), kind=kCustom, calls=%fused_computation.3 | custom fusion | bytes 2621568 | tf_op jit(solution)/shard_map/gather | solution.py:68
  51.0 1.5 %copy.27 = f32[16,4,2560]{2,1,0:T(4,128)S(1)} copy(f32[16,4,2560]{2,0,1:T(8,128)} %get-tuple-element.16) | data formatting | bytes 1310720 | tf_op jit(solution)/shard_map/sub | solution.py:43
  52.5 2.3 %gather_fusion = f32[32,4,2560]{2,1,0:T(4,128)} fusion(f32[16,4,2560]{2,1,0:T(4,128)S(1)} %copy.27, s32[1024]{0:T(1024)S(1)} %get-tuple-element.21), kind=kCustom, calls=%fused_computation | custom fusion | bytes 2621568 | tf_op jit(solution)/shard_map/gather | solution.py:65
  54.8 2.3 %gather_fusion.1 = f32[32,4,2560]{2,1,0:T(4,128)} fusion(f32[16,4,2560]{2,1,0:T(4,128)S(1)} %copy.27, s32[1024]{0:T(1024)S(1)} %get-tuple-element.20), kind=kCustom, calls=%fused_computation.1 | custom fusion | bytes 2621568 | tf_op jit(solution)/shard_map/gather | solution.py:67
  57.1 3.6 %add_reduce_fusion = (f32[32,2560]{1,0:T(8,128)S(1)}, f32[32,2560]{1,0:T(8,128)S(1)}) fusion(f32[32,4,2560]{2,1,0:T(4,128)S(1)} %gather_fusion.2, f32[32,4,2560]{2,1,0:T(4,128)S(1)} %gather_fusion.3, f32[32,4,2560]{2,1,0:T(4,128)} %gather_fusion, f32[32,4,2560]{2,1,0:T(4,128)} %gather_fusion.1), kind=kLoop, calls=%fused_computation.12 | loop fusion | flops 2457600 | bytes 5898240 | tf_op jit(solution)/shard_map/reduce_sum | solution.py:24
  60.8 0.7 fusion.4
  61.5 0.7 fusion.3
  62.2 0.2 convolution_bitcast_fusion
  62.5 0.1 copy.31
  62.6 15.2 %all_to_all.36 = f32[64,3,1,128]{3,2,1,0:T(1,128)S(1)} all-to-all(f32[64,3,1,128]{3,2,1,0:T(1,128)S(1)} %copy.31), channel_id=1, replica_groups=mesh['groups'=2,'date'=16] {'date'}, dimensions={0} | all-to-all | bytes 196608 | tf_op jit(solution)/shard_map/all_to_all | solution.py:89
  77.8 0.6 slice_bitcast_fusion
  78.5 0.6 copy.33
  (8 shorter events, 0.1 us)
Async XLA Ops:
  4.0 7.5 %copy-start.2 = (s32[32,2]{0,1:T(2,128)S(1)}, s32[32,2]{0,1:T(2,128)}, u32[]{:S(2)}) copy-start(s32[32,2]{0,1:T(2,128)} %param.8) | copy-start | bytes 772
  4.0 7.6 %copy-start.3 = (s32[32,1]{0,1:T(1,128)S(1)}, s32[32,1]{0,1:T(1,128)}, u32[]{:S(2)}) copy-start(s32[32,1]{0,1:T(1,128)} %param.9) | copy-start | bytes 388
  4.0 34.9 %all-to-all-start = ((f32[1,2,64,2560]{3,1,0,2:T(2,128)}), f32[1,2,64,2560]{3,1,0,2:T(2,128)S(1)}, u32[]{:S(2)}, u32[]{:S(2)}) async-start(f32[1,2,64,2560]{3,1,0,2:T(2,128)} %copy.25), calls=%async_computation | async-start | bytes 2621440 | tf_op jit(solution)/shard_map/all_to_all | solution.py:61
  39.0 0.8 copy-start
  39.0 0.8 copy-start.1
where the time goes:
time: 79.5 us; the launch traced here: 79.1 us
  waiting for transfers between devices  27.1 us (34%)
  local copies, waits for them, and re-layouts  15.9 us (20%)
  blocking collectives  15.2 us (19%)
  other arithmetic  10.3 us (13%)
  starting transfers between devices  7.52 us (9%)
  matrix products  2.33 us (3%)
    all_to_all x1, waiting for transfers between devices, body(): lax.all_to_all(images, 'date', split_axis=2, concat_axis=0, tiled=True)  27.1 us
    all_to_all x1, blocking collectives, body(): lax.all_to_all(buffer, 'date', split_axis=0, concat_axis=2, tiled=True)  15.2 us
    all_to_all x1, starting transfers between devices, body(): lax.all_to_all(images, 'date', split_axis=2, concat_axis=0, tiled=True)  7.52 us
    reduce_sum x2, other arithmetic, multilook(): jnp.sum(values.reshape(values_shape[:-2] + (row_count // LOOK_ROWS, LOOK_...  6.5 us
    unnamed x10, local copies, waits for them, and re-layouts  4.05 us
    sub x1, other arithmetic, flatten_phase(): real_part = images[:, 0] * cosine - images[:, 1] * sine_part  3.42 us
    gather x1, local copies, waits for them, and re-layouts, body(): real_part[second_index]  2.33 us
    gather x1, local copies, waits for them, and re-layouts, body(): real_part[first_index]  2.31 us
  transfers between devices with their start and end apart: 1, of which 1 were waited for; matrix products, arithmetic and copies ran while one was open for 0% of the time, Pallas kernels for 0%

commit v1 on v0

v1 whole, which is shorter than its diff:
```python
import functools

import jax
import jax.numpy as jnp
from jax import lax
from jax.experimental import pallas as pl
from jax.experimental.pallas import tpu as pltpu
from jax.sharding import PartitionSpec as P

LOOK_ROWS = 4
LOOK_COLS = 20
BAND = 4
CAP = 4
EPSILON = 1e-06

LANES = 128
SUB = 8
ROW_SETS = SUB // LOOK_ROWS
KINDS = 3
SLOT_ROWS = KINDS * ROW_SETS
MIB = 1024 * 1024


def box_matrix(columns):
    position = jnp.arange(columns, dtype=jnp.int32)
    target = jnp.arange(columns // LOOK_COLS, dtype=jnp.int32)
    return (position[:, None] // LOOK_COLS == target[None, :]).astype(jnp.bfloat16)


def pack_kernel(half, place_ref, images_ref, packed_ref, *halo_refs):
    side = place_ref[0]
    lane = place_ref[1]
    columns = images_ref.shape[-1]
    upper = lax.broadcasted_iota(jnp.int32, (SUB, columns), 0) < LOOK_ROWS
    for part in range(2):
        for pair in range(half // 2):
            first = images_ref[0, part, pair * SUB : (pair + 1) * SUB, :]
            at = (pair + half // 2) * SUB
            second = images_ref[0, part, at : at + SUB, :]
            spot = slice(part * SUB, (part + 1) * SUB)
            packed_ref[2 * pair, spot, :] = jnp.where(
                upper, first, pltpu.roll(second, LOOK_ROWS, 0)
            )
            packed_ref[2 * pair + 1, spot, :] = jnp.where(
                upper, pltpu.roll(first, LOOK_ROWS, 0), second
            )
    for n, halo_ref in enumerate(halo_refs):
        target = n // BAND * BAND + jnp.bitwise_xor(lane, n % BAND)
        halo_ref[...] = packed_ref[jnp.where(side == 0, target, half // 2 + target)]


def table_kernel(blocks, factor_ref, upper_ref, lower_ref, cos_ref, sin_ref):
    groups = factor_ref.shape[0] // SUB

    def block(t, carry):
        column = pl.ds(pl.multiple_of(t * LANES, LANES), LANES)
        for b, phase_ref in enumerate((upper_ref, lower_ref)):
            for line in range(LOOK_ROWS):
                phase = phase_ref[line : line + 1, column]
                for group in range(groups):
                    factor = factor_ref[group * SUB : (group + 1) * SUB, :]
                    x = factor * phase
                    z = x * x
                    s = -1.0 / 39916800.0
                    for c in (362880.0, -5040.0, 120.0, -6.0, 1.0):
                        s = s * z + 1.0 / c
                    s = s * x
                    c = 1.0 / 479001600.0
                    for d in (-3628800.0, 40320.0, -720.0, 24.0, -2.0, 1.0):
                        c = c * z + 1.0 / d
                    twice = s + s
                    at = ((t * SUB + b * LOOK_ROWS + line) * groups + group) * SUB
                    spot = pl.ds(pl.multiple_of(at, SUB), SUB)
                    cos_ref[spot, :] = 1.0 - twice * s
                    sin_ref[spot, :] = twice * c
        return carry

    lax.fori_loop(0, blocks, block, 0)


def pair_kernel(
    half,
    blocks,
    pairs,
    place_ref,
    first_ref,
    second_ref,
    owner_ref,
    own_ref,
    *rest,
):
    halo_refs = rest[:BAND]
    cos_ref, sin_ref, box_ref, out_ref, raw_ref, sum_ref, result_ref, count_ref = rest[
        BAND:
    ]
    tiles = half // SUB
    groups = tiles + 1
    per_part = blocks * SUB
    per_date = 2 * per_part
    side = place_ref[0]
    lane = place_ref[1]
    low = side == 0
    halo_row = side * BAND
    raw_ref[...] = jnp.zeros_like(raw_ref)
    row_index = lax.broadcasted_iota(jnp.int32, (SUB, LANES), 0)
    masks = []
    shifts = []
    for k in range(1, BAND + 1):
        masks.append(
            jnp.where(low, row_index - k, SUB - 1 - k - row_index) >= 0
        )
        shifts.append(jnp.where(low, SUB - k, k))

    def partners(values, edge):
        found = []
        for tile in range(tiles):
            after = values[tile + 1] if tile + 1 < tiles else edge
            before = values[tile - 1] if tile > 0 else edge
            beside = edge if tiles == 1 else jnp.where(low, after, before)
            found.append(
                [
                    pltpu.roll(jnp.where(masks[k], values[tile], beside), shifts[k], 0)
                    for k in range(BAND)
                ]
            )
        return found

    def block(t, carry):
        line_at = pl.multiple_of(t * SUB, SUB)
        column = pl.ds(pl.multiple_of(t * LANES, LANES), LANES)
        for part in range(2):
            for i in range(BAND):
                row = halo_row + jnp.bitwise_xor(lane, i)
                raw_ref[part, pl.ds(row, SUB, stride=SUB), :] = halo_refs[i][
                    pl.ds(part * per_part + line_at, SUB), :
                ]

        def turned(line, group, real, imag):
            at = ((line_at + line) * groups + group) * SUB
            table = pl.ds(pl.multiple_of(at, SUB), SUB)
            cosine = cos_ref[table, :]
            sine_part = sin_ref[table, :]
            return real * cosine - imag * sine_part, real * sine_part + imag * cosine

        for b in range(ROW_SETS):
            sums = {}

            def add(key, term):
                sums[key] = sums[key] + term if key in sums else term

            for line in range(b * LOOK_ROWS, (b + 1) * LOOK_ROWS):
                span = slice(line * SUB, (line + 1) * SUB)
                edge_real, edge_imag = turned(
                    line, tiles, raw_ref[0, span, :], raw_ref[1, span, :]
                )
                add((1 + 2 * BAND, 0), edge_real * edge_real + edge_imag * edge_imag)
                reals = []
                imags = []
                for tile in range(tiles):
                    start = tile * SUB * per_date + line_at + line
                    real, imag = turned(
                        line,
                        tile,
                        own_ref[pl.ds(start, SUB, stride=per_date), :],
                        own_ref[pl.ds(start + per_part, SUB, stride=per_date), :],
                    )
                    add((0, tile), real * real + imag * imag)
                    reals.append(real)
                    imags.append(imag)
                other_reals = partners(reals, edge_real)
                other_imags = partners(imags, edge_imag)
                for tile in range(tiles):
                    for k in range(BAND):
                        other_real = other_reals[tile][k]
                        other_imag = other_imags[tile][k]
                        real = reals[tile]
                        imag = imags[tile]
                        add((1 + 2 * k, tile), real * other_real + imag * other_imag)
                        add((2 + 2 * k, tile), imag * other_real - real * other_imag)
            for (kind, tile), value in sums.items():
                at = (kind * tiles * ROW_SETS + b * (1 if kind > 2 * BAND else tiles) + tile) * SUB
                sum_ref[at : at + SUB, column] = value
        return carry

    lax.fori_loop(0, blocks, block, 0)

    rest_of = sum_ref[...]
    box = box_ref[...]
    looked = None
    for piece in range(3):
        rounded = rest_of.astype(jnp.bfloat16)
        part = jnp.dot(rounded, box, preferred_element_type=jnp.float32)
        looked = part if looked is None else looked + part
        if piece < 2:
            rest_of = rest_of - rounded.astype(jnp.float32)
    looked = looked * (1.0 / (LOOK_ROWS * LOOK_COLS))

    def rows_of(kind, b, tile):
        at = (kind * tiles * ROW_SETS + b * (1 if kind > 2 * BAND else tiles) + tile) * SUB
        return looked[at : at + SUB, :]

    sign = jnp.where(low, 1.0, -1.0)
    for b in range(ROW_SETS):
        powers = [rows_of(0, b, tile) for tile in range(tiles)]
        other_powers = partners(powers, rows_of(1 + 2 * BAND, b, 0))
        for tile in range(tiles):
            for k in range(BAND):
                look_real = rows_of(1 + 2 * k, b, tile)
                look_imag = rows_of(2 + 2 * k, b, tile) * sign
                coherence = jnp.sqrt(
                    look_real * look_real + look_imag * look_imag
                ) / jnp.sqrt((powers[tile] + EPSILON) * (other_powers[tile][k] + EPSILON))
                for kind, value in enumerate((look_real, look_imag, coherence)):
                    at = (k * half + tile * SUB) * SUB + kind * ROW_SETS + b
                    result_ref[pl.ds(at, SUB, stride=SUB), :] = value

    out_ref[...] = jnp.zeros_like(out_ref)

    def clear(o, carry):
        count_ref[o] = 0
        return carry

    lax.fori_loop(0, 2 * half, clear, 0)

    def place(p, carry):
        owner = owner_ref[p]
        taken = count_ref[owner]
        count_ref[owner] = taken + 1
        first = first_ref[p]
        second = second_ref[p]
        mine = jnp.where(low, first < half, second >= half)

        @pl.when(mine)
        def _():
            own = jnp.where(low, first, second - half)
            at = pl.multiple_of(((second - first - 1) * half + own) * SUB, SUB)
            out_ref[pl.ds((owner * CAP + taken) * SLOT_ROWS, SLOT_ROWS), :] = (
                result_ref[pl.ds(at, SUB), :][:SLOT_ROWS]
            )

        return carry

    lax.fori_loop(0, pairs, place, 0)


def collect_kernel(half, got_ref, look_ref, coherence_ref):
    per_device = CAP * SLOT_ROWS
    for tile in range(half // SUB):
        for slot in range(CAP):
            for kind in range(KINDS):
                for b in range(ROW_SETS):
                    at = tile * SUB * per_device + slot * SLOT_ROWS + kind * ROW_SETS + b
                    value = got_ref[pl.ds(at, SUB, stride=per_device), :]
                    at += half * per_device
                    value += got_ref[pl.ds(at, SUB, stride=per_device), :]
                    at = b * half + tile * SUB
                    if kind < 2:
                        look_ref[slot, kind, at : at + SUB, :] = value
                    else:
                        coherence_ref[slot, at : at + SUB, :] = value


def body(images, height_phase, baseline, pair_list, pair_owner):
    devices = lax.axis_size("date")
    half = devices // 2
    me = lax.axis_index("date")
    side = me // half
    lane = me % BAND
    rows, columns = images.shape[2:]
    blocks = columns // LANES
    pairs = pair_list.shape[0]
    tiles = half // SUB
    groups = tiles + 1
    assert images.shape[0] == 1 and rows == SUB * half and half % SUB == 0
    assert columns == blocks * LANES == LANES * LOOK_COLS
    vmem = pl.BlockSpec(memory_space=pltpu.VMEM)
    smem = pl.BlockSpec(memory_space=pltpu.SMEM)
    place = jnp.stack([side, lane]).astype(jnp.int32)

    block = jax.ShapeDtypeStruct((2 * SUB, columns), jnp.float32)
    packed, *edges = pl.pallas_call(
        functools.partial(pack_kernel, half),
        out_shape=[jax.ShapeDtypeStruct((half, 2 * SUB, columns), jnp.float32)]
        + [block] * (half // 2),
        in_specs=[smem, vmem],
        out_specs=[vmem] * (1 + half // 2),
        compiler_params=pltpu.CompilerParams(vmem_limit_bytes=24 * MIB),
        name="pack_lines",
    )(place, images)
    halves = [list(range(half)), list(range(half, devices))]
    own = lax.all_to_all(
        packed, "date", split_axis=0, concat_axis=0, tiled=True, axis_index_groups=halves
    )

    def as_rows(values):
        values = values.reshape(-1, SUB, blocks, LANES)
        return jnp.swapaxes(values, 1, 2).reshape(-1, LANES)

    across = lax.ppermute(
        height_phase, "date", [(k, (k + half) % devices) for k in range(devices)]
    )

    halos = []
    for i in range(BAND):
        arrived = None
        for g in range(half // 2 // BAND):
            steps = []
            for a in range(BAND):
                steps.append((half + a, half // 2 + BAND * g + (a ^ i)))
                steps.append((half - BAND + a, half + BAND * g + (a ^ i)))
            got = lax.ppermute(edges[BAND * g + i], "date", steps)
            arrived = got if arrived is None else arrived + got
        halos.append(as_rows(arrived))

    low = side == 0
    upper_phase = jnp.where(low, height_phase, across)
    lower_phase = jnp.where(low, across, height_phase)
    own_factors = lax.dynamic_slice_in_dim(baseline, side * half, half)
    edge_factors = lax.dynamic_slice_in_dim(
        baseline, jnp.where(low, half, half - SUB), SUB
    )
    factors = 0.5 * jnp.concatenate([own_factors, edge_factors])
    factors = jnp.broadcast_to(factors[:, None], (half + SUB, LANES))
    table = jax.ShapeDtypeStruct((blocks * SUB * groups * SUB, LANES), jnp.float32)
    cosine, sine_part = pl.pallas_call(
        functools.partial(table_kernel, blocks),
        out_shape=[table, table],
        in_specs=[vmem] * 3,
        out_specs=[vmem] * 2,
        compiler_params=pltpu.CompilerParams(vmem_limit_bytes=24 * MIB),
        name="phase_tables",
    )(factors, upper_phase, lower_phase)

    sums = ((1 + 2 * BAND) * tiles + 1) * ROW_SETS * SUB
    slot_rows = devices * CAP * SLOT_ROWS
    buffer = pl.pallas_call(
        functools.partial(pair_kernel, half, blocks, pairs),
        out_shape=jax.ShapeDtypeStruct((slot_rows, LANES), jnp.float32),
        in_specs=[smem] * 4 + [vmem] * (BAND + 4),
        out_specs=vmem,
        scratch_shapes=[
            pltpu.VMEM((2, SUB * SUB, LANES), jnp.float32),
            pltpu.VMEM((sums, columns), jnp.float32),
            pltpu.VMEM((BAND * half * SUB, LANES), jnp.float32),
            pltpu.SMEM((devices,), jnp.int32),
        ],
        compiler_params=pltpu.CompilerParams(vmem_limit_bytes=(12 + 12 * tiles) * MIB),
        name="pair_products",
    )(
        place,
        pair_list[:, 0],
        pair_list[:, 1],
        pair_owner[:, 0],
        as_rows(own.reshape(half * 2, SUB, columns)),
        *halos,
        cosine,
        sine_part,
        box_matrix(columns),
    )
    delivered = lax.all_to_all(
        buffer.reshape(devices, CAP * SLOT_ROWS, LANES),
        "date",
        split_axis=0,
        concat_axis=0,
        tiled=True,
    )
    look_rows = rows // LOOK_ROWS
    return pl.pallas_call(
        functools.partial(collect_kernel, half),
        out_shape=(
            jax.ShapeDtypeStruct((CAP, 2, look_rows, LANES), jnp.float32),
            jax.ShapeDtypeStruct((CAP, look_rows, LANES), jnp.float32),
        ),
        in_specs=[vmem],
        out_specs=(vmem, vmem),
        compiler_params=pltpu.CompilerParams(vmem_limit_bytes=16 * MIB),
        name="collect_slots",
    )(delivered.reshape(slot_rows, LANES))


def solution(mesh):
    in_specs = (
        P(("groups", "date"), None, None, None),
        P(("groups", "date"), None),
        P("groups"),
        P(),
        P(),
    )
    out_specs = (P(("groups", "date"), None, None, None), P(("groups", "date"), None, None))
    return jax.shard_map(body, mesh=mesh, in_specs=in_specs, out_specs=out_specs, check_vma=False)
```

time: 79.5 us -> 53.6 us (0.67)
  waiting for transfers between devices: 27.1 us -> 7.38 us
  local copies, waits for them, and re-layouts: 15.9 us -> 3.85 us
  other arithmetic: 10.3 us -> 1.37 us
  Pallas kernels: 0 us -> 8.69 us
  starting transfers between devices: 7.52 us -> 12.7 us
  blocking collectives: 15.2 us -> 18.4 us
  matrix products: 2.33 us -> 0 us
    all_to_all x1, waiting for transfers between devices: 27.1 us -> 0.01 us  [body(): lax.all_to_all(packed, 'date', split_axis=0, concat_axis=0, tiled=True, a...]
    pallas_call x0 -> x4, Pallas kernels: none -> 8.69 us  [the longest x1 4.75 us: body(): pl.pallas_call(functools.partial(pair_kernel, half, blocks, pairs), out_s...]
    gather x6 -> x0, local copies, waits for them, and re-layouts: 8.45 us -> none  [the longest x1 2.33 us: body(): real_part[second_index]]
    ppermute x0 -> x5, waiting for transfers between devices: none -> 7.37 us  [the longest x1 7.36 us: body(): lax.ppermute(height_phase, 'date', [(k, (k + half) % devices) for k in ra...]
    ppermute x0 -> x5, starting transfers between devices: none -> 7.31 us  [the longest x4 4.65 us: body(): got = lax.ppermute(edges[BAND * g + i], 'date', steps)]
    reduce_sum x4 -> x0, other arithmetic: 6.78 us -> none  [the longest x2 6.5 us: multilook(): jnp.sum(values.reshape(values_shape[:-2] + (row_count // LOOK_ROWS, LOOK_...]
    sub x2 -> x0, other arithmetic: 3.43 us -> none  [the longest x1 3.42 us: flatten_phase(): real_part = images[:, 0] * cosine - images[:, 1] * sine_part]
    all_to_all x1, blocking collectives: 15.2 us -> 18.4 us  [body(): lax.all_to_all(buffer.reshape(devices, CAP * SLOT_ROWS, LANES), 'date', s...]
  transfers between devices with their start and end apart: 1 -> 6, of which waited for: 1 -> 1; matrix products, arithmetic and copies ran while one was open for 0% -> 3% of each run, Pallas kernels for 0% -> 3%
where the time goes in v1:
time: 53.6 us; the launch traced here: 53.1 us
  blocking collectives  18.4 us (34%)
  starting transfers between devices  12.7 us (24%)
  Pallas kernels  8.69 us (16%)
  waiting for transfers between devices  7.38 us (14%)
  local copies, waits for them, and re-layouts  3.85 us (7%)
  other arithmetic  1.37 us (3%)
  between operations  0.77 us (1%)
    all_to_all x1, blocking collectives, body(): lax.all_to_all(buffer.reshape(devices, CAP * SLOT_ROWS, LANES), 'date', s...  18.4 us
    ppermute x1, waiting for transfers between devices, body(): lax.ppermute(height_phase, 'date', [(k, (k + half) % devices) for k in ra...  7.36 us
    all_to_all x1, starting transfers between devices, body(): lax.all_to_all(packed, 'date', split_axis=0, concat_axis=0, tiled=True, a...  5.4 us
    pallas_call x1, Pallas kernels, body(): pl.pallas_call(functools.partial(pair_kernel, half, blocks, pairs), out_s...  4.75 us
    ppermute x4, starting transfers between devices, body(): got = lax.ppermute(edges[BAND * g + i], 'date', steps)  4.65 us
    unnamed x14, local copies, waits for them, and re-layouts  3.7 us
    ppermute x1, starting transfers between devices, body(): lax.ppermute(height_phase, 'date', [(k, (k + half) % devices) for k in ra...  2.65 us
    pallas_call x1, Pallas kernels, body(): pl.pallas_call(functools.partial(pack_kernel, half), out_shape=[jax.Shape...  1.9 us
  transfers between devices with their start and end apart: 6, of which 1 were waited for; matrix products, arithmetic and copies ran while one was open for 3% of the time, Pallas kernels for 3%

profile of v1, /device:TPU:0, one launch (start us, length us, event | category | flops | bytes accessed | tf_op | source)
XLA Modules:
  0.0 53.1 jit_solution(17892939094349423127)
XLA Ops:
  0.7 0.1 pad_add_fusion.place_ref
  0.7 0.0 copy-start
  0.7 1.3 %copy-done = f32[1,2,64,2560]{3,2,1,0:T(8,128)S(1)} copy-done((f32[1,2,64,2560]{3,2,1,0:T(8,128)S(1)}, f32[1,2,64,2560]{3,2,1,0:T(8,128)}, u32[]{:S(2)}) %copy-start) | copy-done | bytes 1310744
  2.0 1.9 %pack_lines.1 = (f32[8,16,2560]{2,1,0:T(8,128)}, f32[16,2560]{1,0:T(8,128)}, f32[16,2560]{1,0:T(8,128)}, f32[16,2560]{1,0:T(8,128)}, f32[16,2560]{1,0:T(8,128)}) custom-call(s32[2]{0:T(128)S(1)} %pad_add_fusion.place_ref, f32[1,2,64,2560]{3,2,1,0:T(8,128)S(1)} %copy-done), custom_call_target="tpu_custom_call" | custom-call | tf_op jit(solution)/shard_map/pack_lines/pallas_call | solution.py:281
  3.9 0.0 copy-start.4
  3.9 0.0 copy-start.5
  4.0 0.0 copy-start.6
  4.0 0.0 copy-start.3
  4.0 5.4 %all-to-all-start = ((f32[8,16,2560]{2,1,0:T(8,128)}), f32[8,16,2560]{2,1,0:T(8,128)S(1)}, u32[]{:S(2)}, u32[]{:S(2)}) async-start(f32[8,16,2560]{2,1,0:T(8,128)} %get-tuple-element.9), calls=%async_computation | async-start | bytes 2621440 | tf_op jit(solution)/shard_map/all_to_all | solution.py:291
  9.4 0.0 copy-done.4
  9.4 2.7 %collective-permute-start.4 = (f32[4,2560]{1,0:T(4,128)S(1)}, f32[4,2560]{1,0:T(4,128)S(1)}, u32[]{:S(2)}, u32[]{:S(2)}) collective-permute-start(f32[4,2560]{1,0:T(4,128)S(1)} %copy-done.4), channel_id=1, source_target_pairs={{0,8},{1,9},{2,10},{3,11},{4,12},{5,13},{6,14},{7,15},{8,0},{9,1},... | collective-permute-start | bytes 122888 | tf_op jit(solution)/shard_map/ppermute | solution.py:299
  12.0 0.7 %collective-permute-start = (f32[16,2560]{1,0:T(8,128)}, f32[16,2560]{1,0:T(8,128)S(1)}, u32[]{:S(2)}, u32[]{:S(2)}) collective-permute-start(f32[16,2560]{1,0:T(8,128)} %get-tuple-element.10), channel_id=1, source_target_pairs={{8,4},{4,8},{9,5},{5,9},{10,6},{6,10},{11,7},{7,11},{24,20},{20,24... | collective-permute-start | bytes 491528 | tf_op jit(solution)/shard_map/ppermute | solution.py:311
  12.7 1.3 %collective-permute-start.1 = (f32[16,2560]{1,0:T(8,128)}, f32[16,2560]{1,0:T(8,128)}, u32[]{:S(2)}, u32[]{:S(2)}) collective-permute-start(f32[16,2560]{1,0:T(8,128)} %get-tuple-element.11), channel_id=1, source_target_pairs={{8,5},{4,9},{9,4},{5,8},{10,7},{6,11},{11,6},{7,10},{24,21},{20,25... | collective-permute-start | bytes 491528 | tf_op jit(solution)/shard_map/ppermute | solution.py:311
  14.0 1.3 %collective-permute-start.2 = (f32[16,2560]{1,0:T(8,128)}, f32[16,2560]{1,0:T(8,128)}, u32[]{:S(2)}, u32[]{:S(2)}) collective-permute-start(f32[16,2560]{1,0:T(8,128)} %get-tuple-element.12), channel_id=1, source_target_pairs={{8,6},{4,10},{9,7},{5,11},{10,4},{6,8},{11,5},{7,9},{24,22},{20,26... | collective-permute-start | bytes 491528 | tf_op jit(solution)/shard_map/ppermute | solution.py:311
  15.4 1.3 %collective-permute-start.3 = (f32[16,2560]{1,0:T(8,128)}, f32[16,2560]{1,0:T(8,128)}, u32[]{:S(2)}, u32[]{:S(2)}) collective-permute-start(f32[16,2560]{1,0:T(8,128)} %get-tuple-element.13), channel_id=1, source_target_pairs={{8,7},{4,11},{9,6},{5,10},{10,5},{6,9},{11,4},{7,8},{24,23},{20,27... | collective-permute-start | bytes 491528 | tf_op jit(solution)/shard_map/ppermute | solution.py:311
  16.7 0.0 copy-done.5
  16.7 0.1 fusion.4
  16.8 0.0 copy-done.6
  16.8 1.2 %fusion.rest_6_ = bf16[2560,128]{1,0:T(8,128)(2,1)S(1)} fusion(s32[2560]{0:T(1024)S(1)} %add_select_fusion), kind=kLoop, calls=%fused_computation.1 | loop fusion | flops 655360 | bytes 665600 | tf_op jit(solution)/shard_map/convert_element_type | solution.py:27
  18.0 0.1 maximum_multiply_fusion
  18.1 7.4 %collective-permute-done.4 = f32[4,2560]{1,0:T(4,128)S(1)} collective-permute-done((f32[4,2560]{1,0:T(4,128)S(1)}, f32[4,2560]{1,0:T(4,128)S(1)}, u32[]{:S(2)}, u32[]{:S(2)}) %collective-permute-start.4) | collective-permute-done | bytes 40992 | tf_op jit(solution)/shard_map/ppermute | solution.py:299
  25.5 0.1 broadcast_in_dim.2.factor_ref
  25.5 1.4 %phase_tables.1 = (f32[2560,128]{1,0:T(8,128)S(1)}, f32[2560,128]{1,0:T(8,128)S(1)}) custom-call(f32[16,128]{1,0:T(8,128)S(1)} %broadcast_in_dim.2.factor_ref, f32[4,2560]{1,0:T(4,128)S(1)} %get-tuple-element.17.upper_ref, f32[4,2560]{1,0:T(4,128)S(1)} %get-tuple-element.16.lower_ref), custom_call_target="tpu_custom_call" | custom-call | tf_op jit(solution)/shard_map/phase_tables/pallas_call | solution.py:325
  26.9 0.0 copy-start.1
  26.9 1.1 %copy-done.1 = f32[2560,128]{1,0:T(8,128)} copy-done((f32[2560,128]{1,0:T(8,128)}, f32[2560,128]{1,0:T(8,128)S(1)}, u32[]{:S(2)}) %copy-start.1) | copy-done | bytes 1310744
  28.0 0.0 collective-permute-done
  28.0 0.0 collective-permute-done.1
  28.0 0.0 collective-permute-done.2
  28.0 0.0 collective-permute-done.3
  28.0 0.0 all-to-all-done
  28.0 0.0 copy-done.3
  28.0 0.0 copy-start.2
  28.0 1.3 %copy-done.2 = f32[2560,128]{1,0:T(8,128)S(1)} copy-done((f32[2560,128]{1,0:T(8,128)S(1)}, f32[2560,128]{1,0:T(8,128)}, u32[]{:S(2)}) %copy-start.2) | copy-done | bytes 1310744
  29.3 4.8 %pair_products.1 = f32[384,128]{1,0:T(8,128)S(1)} custom-call(s32[2]{0:T(128)S(1)} %pad_add_fusion.place_ref, s32[32]{0:T(128)S(1)} %get-tuple-element.19.first_ref, s32[32]{0:T(128)S(1)} %get-tuple-element.18.second_ref, s32[32]{0:T(128)S(1)} %bitcast.38, f32[2560,128]{1,0:T(8,128)S(1)} %bitcast.34, f32[320,128]{1,0:T(8,128)S(1)} %bitcast.37, ...), custom_call_target="tpu_custom_call" | custom-call | tf_op jit(solution)/shard_map/pair_products/pallas_call | solution.py:336
  34.1 18.4 %all_to_all.10 = f32[16,24,128]{2,1,0:T(8,128)S(1)} all-to-all(f32[16,24,128]{2,1,0:T(8,128)S(1)} %bitcast.35), channel_id=1, replica_groups=mesh['groups'=2,'date'=16] {'date'}, dimensions={0} | all-to-all | bytes 393216 | tf_op jit(solution)/shard_map/all_to_all | solution.py:360
  52.5 0.7 %collect_slots.1 = (f32[4,2,16,128]{3,2,1,0:T(8,128)}, f32[4,16,128]{2,1,0:T(8,128)}) custom-call(f32[384,128]{1,0:T(8,128)S(1)} %bitcast.36), custom_call_target="tpu_custom_call" | custom-call | tf_op jit(solution)/shard_map/collect_slots/pallas_call | solution.py:368
  (3 shorter events, 0.0 us)
Async XLA Ops:
  0.7 1.3 %copy-start = (f32[1,2,64,2560]{3,2,1,0:T(8,128)S(1)}, f32[1,2,64,2560]{3,2,1,0:T(8,128)}, u32[]{:S(2)}) copy-start(f32[1,2,64,2560]{3,2,1,0:T(8,128)} %images_ref.1) | copy-start | bytes 3932164
  3.9 5.4 %copy-start.4 = (f32[4,2560]{1,0:T(4,128)S(1)}, f32[4,2560]{1,0:T(4,128)}, u32[]{:S(2)}) copy-start(f32[4,2560]{1,0:T(4,128)} %param.6) | copy-start | bytes 122884
  3.9 12.7 %copy-start.5 = (f32[16]{0:T(128)S(1)}, f32[16]{0:T(128)}, u32[]{:S(2)}) copy-start(f32[16]{0:T(128)} %param.7) | copy-start | bytes 196
  4.0 12.8 %copy-start.6 = (s32[32,2]{0,1:T(2,128)S(1)}, s32[32,2]{0,1:T(2,128)}, u32[]{:S(2)}) copy-start(s32[32,2]{0,1:T(2,128)} %param.8) | copy-start | bytes 772
  4.0 24.1 %copy-start.3 = (s32[32,1]{0,1:T(1,128)S(1)}, s32[32,1]{0,1:T(1,128)}, u32[]{:S(2)}) copy-start(s32[32,1]{0,1:T(1,128)} %param.9) | copy-start | bytes 388
  4.0 24.0 %all-to-all-start = ((f32[8,16,2560]{2,1,0:T(8,128)}), f32[8,16,2560]{2,1,0:T(8,128)S(1)}, u32[]{:S(2)}, u32[]{:S(2)}) async-start(f32[8,16,2560]{2,1,0:T(8,128)} %get-tuple-element.9), calls=%async_computation | async-start | bytes 2621440 | tf_op jit(solution)/shard_map/all_to_all | solution.py:291
  9.4 16.1 %collective-permute-start.4 = (f32[4,2560]{1,0:T(4,128)S(1)}, f32[4,2560]{1,0:T(4,128)S(1)}, u32[]{:S(2)}, u32[]{:S(2)}) collective-permute-start(f32[4,2560]{1,0:T(4,128)S(1)} %copy-done.4), channel_id=1, source_target_pairs={{0,8},{1,9},{2,10},{3,11},{4,12},{5,13},{6,14},{7,15},{8,0},{9,1},... | collective-permute-start | bytes 122888 | tf_op jit(solution)/shard_map/ppermute | solution.py:299
  12.0 16.0 %collective-permute-start = (f32[16,2560]{1,0:T(8,128)}, f32[16,2560]{1,0:T(8,128)S(1)}, u32[]{:S(2)}, u32[]{:S(2)}) collective-permute-start(f32[16,2560]{1,0:T(8,128)} %get-tuple-element.10), channel_id=1, source_target_pairs={{8,4},{4,8},{9,5},{5,9},{10,6},{6,10},{11,7},{7,11},{24,20},{20,24... | collective-permute-start | bytes 491528 | tf_op jit(solution)/shard_map/ppermute | solution.py:311
  12.7 15.3 %collective-permute-start.1 = (f32[16,2560]{1,0:T(8,128)}, f32[16,2560]{1,0:T(8,128)}, u32[]{:S(2)}, u32[]{:S(2)}) collective-permute-start(f32[16,2560]{1,0:T(8,128)} %get-tuple-element.11), channel_id=1, source_target_pairs={{8,5},{4,9},{9,4},{5,8},{10,7},{6,11},{11,6},{7,10},{24,21},{20,25... | collective-permute-start | bytes 491528 | tf_op jit(solution)/shard_map/ppermute | solution.py:311
  14.0 14.0 %collective-permute-start.2 = (f32[16,2560]{1,0:T(8,128)}, f32[16,2560]{1,0:T(8,128)}, u32[]{:S(2)}, u32[]{:S(2)}) collective-permute-start(f32[16,2560]{1,0:T(8,128)} %get-tuple-element.12), channel_id=1, source_target_pairs={{8,6},{4,10},{9,7},{5,11},{10,4},{6,8},{11,5},{7,9},{24,22},{20,26... | collective-permute-start | bytes 491528 | tf_op jit(solution)/shard_map/ppermute | solution.py:311
  15.4 12.6 %collective-permute-start.3 = (f32[16,2560]{1,0:T(8,128)}, f32[16,2560]{1,0:T(8,128)}, u32[]{:S(2)}, u32[]{:S(2)}) collective-permute-start(f32[16,2560]{1,0:T(8,128)} %get-tuple-element.13), channel_id=1, source_target_pairs={{8,7},{4,11},{9,6},{5,10},{10,5},{6,9},{11,4},{7,8},{24,23},{20,27... | collective-permute-start | bytes 491528 | tf_op jit(solution)/shard_map/ppermute | solution.py:311
  26.9 1.1 %copy-start.1 = (f32[2560,128]{1,0:T(8,128)}, f32[2560,128]{1,0:T(8,128)S(1)}, u32[]{:S(2)}) copy-start(f32[2560,128]{1,0:T(8,128)S(1)} %get-tuple-element.15.rest_5_) | copy-start | bytes 3932164
  28.0 1.3 %copy-start.2 = (f32[2560,128]{1,0:T(8,128)S(1)}, f32[2560,128]{1,0:T(8,128)}, u32[]{:S(2)}) copy-start(f32[2560,128]{1,0:T(8,128)} %copy-done.1) | copy-start | bytes 3932164

commit v2 on v1

v2 whole, which is shorter than its diff:
```python
import functools

import jax
import jax.numpy as jnp
from jax import lax
from jax.experimental import pallas as pl
from jax.experimental.pallas import tpu as pltpu
from jax.sharding import PartitionSpec as P

LOOK_ROWS = 4
LOOK_COLS = 20
BAND = 4
CAP = 4
EPSILON = 1e-06

LANES = 128
SUB = 8
ROW_SETS = SUB // LOOK_ROWS
KINDS = 3
SLOT_ROWS = KINDS * ROW_SETS
BOX_PARTS = 4
MIB = 1024 * 1024


SINE = (1.0, -0.1666666567325592, 0.00833327230066061, -0.00019829686789307743, 2.665147349034669e-06)
COSINE = (1.0, -0.49999988079071045, 0.041666001081466675, -0.001387619529850781, 2.3807961042621173e-05)


def cosine_and_sine(x):
    z = x * x
    s = SINE[-1]
    for c in SINE[-2::-1]:
        s = s * z + c
    s = s * x
    c = COSINE[-1]
    for d in COSINE[-2::-1]:
        c = c * z + d
    twice = s + s
    return 1.0 - twice * s, twice * c


def edge_kernel(half, packed_ref, *rest):
    edge_refs = rest[: half // 2]
    sem = rest[half // 2]
    me = lax.axis_index("date")
    lane = lax.rem(me, BAND)
    first = jnp.where(me < half, 0, half // 2)
    arriving = []
    for n, edge_ref in enumerate(edge_refs):
        target = first + n // BAND * BAND + jnp.bitwise_xor(lane, n % BAND)
        arriving.append(
            pltpu.make_async_copy(packed_ref.at[target], edge_ref, sem.at[n])
        )
        arriving[-1].start()
    for copy in arriving:
        copy.wait()


def pair_kernel(half, blocks, pairs, place_ref, factor_ref, phase_ref, own_ref, *rest):
    halo_refs = rest[:BAND]
    out_ref, raw_ref, sum_ref, box_ref, result_ref = rest[BAND:]
    tiles = half // SUB
    per_part = blocks * SUB
    per_date = 2 * per_part
    side = place_ref[0]
    lane = place_ref[1]
    low = side == 0
    row_index = lax.broadcasted_iota(jnp.int32, (SUB, LANES), 0)
    masks = []
    shifts = []
    for k in range(1, BAND + 1):
        masks.append(
            jnp.where(low, row_index - k, SUB - 1 - k - row_index) >= 0
        )
        shifts.append(jnp.where(low, SUB - k, k))

    def partners(values, edge):
        found = []
        for tile in range(tiles):
            after = values[tile + 1] if tile + 1 < tiles else edge
            before = values[tile - 1] if tile > 0 else edge
            beside = edge if tiles == 1 else jnp.where(low, after, before)
            found.append(
                [
                    pltpu.roll(jnp.where(masks[k], values[tile], beside), shifts[k], 0)
                    for k in range(BAND)
                ]
            )
        return found

    box_columns = box_ref.shape[0]
    offset = lax.broadcasted_iota(
        jnp.int32, (box_columns, LANES), 0
    ) - LOOK_COLS * lax.broadcasted_iota(jnp.int32, (box_columns, LANES), 1)
    inside = jnp.where((offset >= 0) & (offset < LOOK_COLS), 1.0, 0.0)
    box_ref[...] = inside.astype(jnp.bfloat16)

    def turned(angle, real, imag):
        cosine, sine_part = cosine_and_sine(angle)
        return real * cosine - imag * sine_part, real * sine_part + imag * cosine

    first_row = row_index < BAND
    to_even = SUB // 2 * side
    to_odd = SUB // 2 - to_even
    edge_kind = 1 + 2 * BAND

    def block(t, carry):
        line_at = pl.multiple_of(t * SUB, SUB)
        column = pl.ds(pl.multiple_of(t * LANES, LANES), LANES)
        for part in range(2):
            for i in range(BAND):
                row = jnp.bitwise_xor(lane, i)
                raw_ref[part, pl.ds(row, SUB, stride=BAND), :] = halo_refs[i][
                    pl.ds(part * per_part + line_at, SUB), :
                ]
        for b in range(ROW_SETS):
            sums = {}

            def add(key, term):
                sums[key] = sums[key] + term if key in sums else term

            for even in range(b * LOOK_ROWS, (b + 1) * LOOK_ROWS, 2):
                phases = [phase_ref[line : line + 1, column] for line in (even, even + 1)]
                span = slice(even * BAND, even * BAND + SUB)
                edge = turned(
                    factor_ref[tiles * SUB :, :] * jnp.where(first_row, *phases),
                    raw_ref[0, span, :],
                    raw_ref[1, span, :],
                )
                add((edge_kind, 0), edge[0] * edge[0] + edge[1] * edge[1])
                for line in (even, even + 1):
                    to_place = to_even if line == even else to_odd
                    edge_real, edge_imag = [pltpu.roll(v, to_place, 0) for v in edge]
                    reals = []
                    imags = []
                    for tile in range(tiles):
                        start = tile * SUB * per_date + line_at + line
                        real, imag = turned(
                            factor_ref[tile * SUB : (tile + 1) * SUB, :]
                            * phases[line - even],
                            own_ref[pl.ds(start, SUB, stride=per_date), :],
                            own_ref[pl.ds(start + per_part, SUB, stride=per_date), :],
                        )
                        add((0, tile), real * real + imag * imag)
                        reals.append(real)
                        imags.append(imag)
                    other_reals = partners(reals, edge_real)
                    other_imags = partners(imags, edge_imag)
                    for tile in range(tiles):
                        for k in range(BAND):
                            other_real = other_reals[tile][k]
                            other_imag = other_imags[tile][k]
                            real = reals[tile]
                            imag = imags[tile]
                            add((1 + 2 * k, tile), real * other_real + imag * other_imag)
                            add((2 + 2 * k, tile), imag * other_real - real * other_imag)
            for (kind, tile), value in sums.items():
                at = sum_row(kind, b, tile)
                sum_ref[at : at + SUB, column] = value
        return carry

    def sum_row(kind, b, tile):
        return (kind * tiles * ROW_SETS + b * (1 if kind == edge_kind else tiles) + tile) * SUB

    lax.fori_loop(0, blocks, block, 0)

    box = box_ref[...]
    looked = None
    for part in range(sum_ref.shape[1] // box_columns):
        rest_of = sum_ref[:, part * box_columns : (part + 1) * box_columns]
        parts = None
        for piece in range(3):
            rounded = rest_of.astype(jnp.bfloat16)
            value = jnp.dot(rounded, box, preferred_element_type=jnp.float32)
            parts = value if parts is None else parts + value
            if piece < 2:
                rest_of = rest_of - rounded.astype(jnp.float32)
        if part:
            parts = pltpu.roll(parts, part * (box_columns // LOOK_COLS), 1)
        looked = parts if looked is None else looked + parts
    looked = looked * (1.0 / (LOOK_ROWS * LOOK_COLS))

    def rows_of(kind, b, tile):
        at = sum_row(kind, b, tile)
        return looked[at : at + SUB, :]

    sign = jnp.where(low, 1.0, -1.0)
    for b in range(ROW_SETS):
        powers = [rows_of(0, b, tile) for tile in range(tiles)]
        edge_power = rows_of(edge_kind, b, 0)
        other_powers = partners(powers, edge_power + pltpu.roll(edge_power, SUB // 2, 0))
        for tile in range(tiles):
            for k in range(BAND):
                look_real = rows_of(1 + 2 * k, b, tile)
                look_imag = rows_of(2 + 2 * k, b, tile) * sign
                coherence = jnp.sqrt(
                    look_real * look_real + look_imag * look_imag
                ) / jnp.sqrt((powers[tile] + EPSILON) * (other_powers[tile][k] + EPSILON))
                for kind, value in enumerate((look_real, look_imag, coherence)):
                    at = (k * half + tile * SUB) * SUB + kind * ROW_SETS + b
                    result_ref[pl.ds(at, SUB, stride=SUB), :] = value

    out_ref[...] = jnp.zeros_like(out_ref)
    result_ref[BAND * half * SUB :, :] = jnp.zeros((SUB, LANES), jnp.float32)
    for p in range(pairs):
        taken = pl.multiple_of(place_ref[2 + pairs + p] * SUB, SUB)
        out_ref[pl.ds(place_ref[2 + p] * SLOT_ROWS, SLOT_ROWS), :] = result_ref[
            pl.ds(taken, SUB), :
        ][:SLOT_ROWS]


def collect_kernel(half, got_ref, look_ref, coherence_ref):
    per_device = CAP * SLOT_ROWS
    for tile in range(half // SUB):
        for slot in range(CAP):
            for kind in range(KINDS):
                for b in range(ROW_SETS):
                    at = tile * SUB * per_device + slot * SLOT_ROWS + kind * ROW_SETS + b
                    value = got_ref[pl.ds(at, SUB, stride=per_device), :]
                    at += half * per_device
                    value += got_ref[pl.ds(at, SUB, stride=per_device), :]
                    spot = pl.ds(tile * SUB * ROW_SETS + b, SUB, stride=ROW_SETS)
                    if kind < 2:
                        look_ref[slot, kind, spot, :] = value
                    else:
                        coherence_ref[slot, spot, :] = value


def body(images, height_phase, baseline, pair_list, pair_owner):
    devices = lax.axis_size("date")
    half = devices // 2
    me = lax.axis_index("date")
    side = me // half
    lane = me % BAND
    rows, columns = images.shape[2:]
    blocks = columns // LANES
    pairs = pair_list.shape[0]
    tiles = half // SUB
    assert images.shape[0] == 1 and rows == SUB * half and half % SUB == 0
    assert columns == blocks * LANES == LANES * LOOK_COLS and blocks % BOX_PARTS == 0
    vmem = pl.BlockSpec(memory_space=pltpu.VMEM)
    smem = pl.BlockSpec(memory_space=pltpu.SMEM)
    place = jnp.stack([side, lane]).astype(jnp.int32)

    beside = lax.ppermute(height_phase, "date", [(k, k ^ 1) for k in range(devices)])

    packed = jnp.swapaxes(images[0].reshape(2, half, SUB, columns), 0, 1)
    packed = packed.reshape(half, 2 * SUB, columns)
    edges = pl.pallas_call(
        functools.partial(edge_kernel, half),
        out_shape=[jax.ShapeDtypeStruct((2 * SUB, columns), jnp.float32)] * (half // 2),
        in_specs=[pl.BlockSpec(memory_space=pltpu.HBM)],
        out_specs=[vmem] * (half // 2),
        scratch_shapes=[pltpu.SemaphoreType.DMA((half // 2,))],
        name="edge_lines",
    )(packed)
    halves = [list(range(half)), list(range(half, devices))]
    own = lax.all_to_all(
        packed, "date", split_axis=0, concat_axis=0, tiled=True, axis_index_groups=halves
    )

    def as_rows(values):
        values = values.reshape(-1, SUB, blocks, LANES)
        return jnp.swapaxes(values, 1, 2).reshape(-1, LANES)

    halos = []
    for i in range(BAND):
        arrived = None
        for g in range(half // 2 // BAND):
            steps = []
            for a in range(BAND):
                steps.append((half + a, half // 2 + BAND * g + (a ^ i)))
                steps.append((half - BAND + a, half + BAND * g + (a ^ i)))
            got = lax.ppermute(edges[BAND * g + i], "date", steps)
            arrived = got if arrived is None else arrived + got
        halos.append(as_rows(arrived))

    low = side == 0
    both = jnp.where(
        me % 2 == 0,
        jnp.concatenate([height_phase, beside]),
        jnp.concatenate([beside, height_phase]),
    )
    phase = lax.ppermute(
        both, "date", [(k, k // 2 + k % 2 * half) for k in range(devices)]
    )
    own_factors = lax.dynamic_slice_in_dim(baseline, side * half, half)
    edge_factors = lax.dynamic_slice_in_dim(
        baseline, jnp.where(low, half, half - BAND), BAND
    )
    factors = 0.5 * jnp.concatenate([own_factors, edge_factors, edge_factors])
    factors = jnp.broadcast_to(factors[:, None], (half + SUB, LANES))
    sums = ((1 + 2 * BAND) * tiles + 1) * ROW_SETS * SUB
    slot_rows = devices * CAP * SLOT_ROWS
    owners = pair_owner[:, 0]
    first = pair_list[:, 0]
    second = pair_list[:, 1]
    earlier = jnp.tril(owners[:, None] == owners[None, :], -1)
    slot = owners * CAP + jnp.sum(earlier.astype(jnp.int32), axis=1)
    held = (second - first - 1) * half + jnp.where(low, first, second - half)
    held = jnp.where(jnp.where(low, first < half, second >= half), held, BAND * half)
    buffer = pl.pallas_call(
        functools.partial(pair_kernel, half, blocks, pairs),
        out_shape=jax.ShapeDtypeStruct((slot_rows, LANES), jnp.float32),
        in_specs=[smem] + [vmem] * (BAND + 3),
        out_specs=vmem,
        scratch_shapes=[
            pltpu.VMEM((2, SUB * BAND, LANES), jnp.float32),
            pltpu.VMEM((sums, columns), jnp.float32),
            pltpu.VMEM((columns // BOX_PARTS, LANES), jnp.bfloat16),
            pltpu.VMEM((BAND * half * SUB + SUB, LANES), jnp.float32),
        ],
        compiler_params=pltpu.CompilerParams(vmem_limit_bytes=(12 + 12 * tiles) * MIB),
        name="pair_products",
    )(
        jnp.concatenate([place, slot, held]),
        factors,
        phase,
        as_rows(own.reshape(half * 2, SUB, columns)),
        *halos,
    )
    delivered = lax.all_to_all(
        buffer.reshape(devices, CAP * SLOT_ROWS, LANES),
        "date",
        split_axis=0,
        concat_axis=0,
        tiled=True,
    )
    look_rows = rows // LOOK_ROWS
    return pl.pallas_call(
        functools.partial(collect_kernel, half),
        out_shape=(
            jax.ShapeDtypeStruct((CAP, 2, look_rows, LANES), jnp.float32),
            jax.ShapeDtypeStruct((CAP, look_rows, LANES), jnp.float32),
        ),
        in_specs=[vmem],
        out_specs=(vmem, vmem),
        compiler_params=pltpu.CompilerParams(vmem_limit_bytes=16 * MIB),
        name="collect_slots",
    )(delivered.reshape(slot_rows, LANES))


def solution(mesh):
    in_specs = (
        P(("groups", "date"), None, None, None),
        P(("groups", "date"), None),
        P("groups"),
        P(),
        P(),
    )
    out_specs = (P(("groups", "date"), None, None, None), P(("groups", "date"), None, None))
    return jax.shard_map(body, mesh=mesh, in_specs=in_specs, out_specs=out_specs, check_vma=False)
```

time: 53.6 us -> 51.8 us (0.966)
  starting transfers between devices: 12.7 us -> 9.29 us
  waiting for transfers between devices: 7.38 us -> 10.6 us
  blocking collectives: 18.4 us -> 20.7 us
  Pallas kernels: 8.69 us -> 6.87 us
  local copies, waits for them, and re-layouts: 3.85 us -> 2.73 us
  other arithmetic: 1.37 us -> 0.38 us
    all_to_all x1, waiting for transfers between devices: 0.01 us -> 10.6 us  [body(): lax.all_to_all(packed, 'date', split_axis=0, concat_axis=0, tiled=True, a...]
    ppermute x1 -> x2, waiting for transfers between devices: 7.36 us -> 0.01 us  [the longest x1 0.01 us: body(): lax.ppermute(height_phase, 'date', [(k, k ^ 1) for k in range(devices)])]
    unnamed x14 -> x10, local copies, waits for them, and re-layouts: 3.7 us -> 1.34 us
    all_to_all x1, blocking collectives: 18.4 us -> 20.7 us  [body(): lax.all_to_all(buffer.reshape(devices, CAP * SLOT_ROWS, LANES), 'date', s...]
    ppermute x4, starting transfers between devices: 4.65 us -> 2.68 us  [body(): got = lax.ppermute(edges[BAND * g + i], 'date', steps)]
    ppermute x1 -> x2, starting transfers between devices: 2.65 us -> 1.22 us  [the longest x1 0.67 us: body(): lax.ppermute(both, 'date', [(k, k // 2 + k % 2 * half) for k in range(dev...]
    pallas_call x2 -> x1, Pallas kernels: 3.27 us -> 2.01 us  [body(): pl.pallas_call(functools.partial(edge_kernel, half), out_shape=[jax.Shape...]
    convert_element_type x1 -> x0, other arithmetic: 1.19 us -> none  [box_matrix(): (position[:, None] // LOOK_COLS == target[None, :]).astype(jnp.bfloat16)]
  transfers between devices with their start and end apart: 6 -> 7, of which waited for: 1 -> 1; matrix products, arithmetic and copies ran while one was open for 3% -> 1% of each run, Pallas kernels for 3% -> 4%
where the time goes in v2:
time: 51.8 us; the launch traced here: 51.4 us
  blocking collectives  20.7 us (40%)
  waiting for transfers between devices  10.6 us (20%)
  starting transfers between devices  9.29 us (18%)
  Pallas kernels  6.87 us (13%)
  local copies, waits for them, and re-layouts  2.73 us (5%)
  between operations  0.8 us (2%)
    all_to_all x1, blocking collectives, body(): lax.all_to_all(buffer.reshape(devices, CAP * SLOT_ROWS, LANES), 'date', s...  20.7 us
    all_to_all x1, waiting for transfers between devices, body(): lax.all_to_all(packed, 'date', split_axis=0, concat_axis=0, tiled=True, a...  10.6 us
    all_to_all x1, starting transfers between devices, body(): lax.all_to_all(packed, 'date', split_axis=0, concat_axis=0, tiled=True, a...  5.39 us
    pallas_call x1, Pallas kernels, body(): pl.pallas_call(functools.partial(pair_kernel, half, blocks, pairs), out_s...  4.19 us
    ppermute x4, starting transfers between devices, body(): got = lax.ppermute(edges[BAND * g + i], 'date', steps)  2.68 us
    pallas_call x1, Pallas kernels, body(): pl.pallas_call(functools.partial(edge_kernel, half), out_shape=[jax.Shape...  2.01 us
    unnamed x10, local copies, waits for them, and re-layouts  1.34 us
    reshape x1, local copies, waits for them, and re-layouts, body(): packed = packed.reshape(half, 2 * SUB, columns)  1.17 us
  transfers between devices with their start and end apart: 7, of which 1 were waited for; matrix products, arithmetic and copies ran while one was open for 1% of the time, Pallas kernels for 4%

profile of v2, /device:TPU:0, one launch (start us, length us, event | category | flops | bytes accessed | tf_op | source)
XLA Modules:
  0.0 51.4 jit_solution(8392719319523407784)
XLA Ops:
  0.6 0.0 copy-start
  0.6 1.3 %copy-done = f32[1,2,64,2560]{3,2,1,0:T(8,128)S(1)} copy-done((f32[1,2,64,2560]{3,2,1,0:T(8,128)S(1)}, f32[1,2,64,2560]{3,2,1,0:T(8,128)}, u32[]{:S(2)}) %copy-start) | copy-done | bytes 1310744
  2.0 1.2 %copy_bitcast_fusion.packed_ref = f32[8,16,2560]{2,1,0:T(8,128)} fusion(f32[1,2,64,2560]{3,2,1,0:T(8,128)S(1)} %copy-done), kind=kLoop, calls=%fused_computation | loop fusion | bytes 2621440 | tf_op jit(solution)/shard_map/reshape | solution.py:248
  3.1 0.0 copy-start.1
  3.1 5.4 %all-to-all-start = ((f32[8,16,2560]{2,1,0:T(8,128)}), f32[8,16,2560]{2,1,0:T(8,128)S(1)}, u32[]{:S(2)}, u32[]{:S(2)}) async-start(f32[8,16,2560]{2,1,0:T(8,128)} %copy_bitcast_fusion.packed_ref), calls=%async_computation | async-start | bytes 2621440 | tf_op jit(solution)/shard_map/all_to_all | solution.py:258
  8.5 0.0 copy-done.1
  8.5 0.0 copy-start.4
  8.5 0.0 copy-start.2
  8.5 0.0 copy-start.3
  8.6 0.6 %collective-permute-start = (f32[4,2560]{1,0:T(4,128)S(1)}, f32[4,2560]{1,0:T(4,128)S(1)}, u32[]{:S(2)}, u32[]{:S(2)}) collective-permute-start(f32[4,2560]{1,0:T(4,128)S(1)} %copy-done.1), channel_id=1, source_target_pairs={{0,1},{1,0},{2,3},{3,2},{4,5},{5,4},{6,7},{7,6},{8,9},{9,8},{10,11... | collective-permute-start | bytes 122888 | tf_op jit(solution)/shard_map/ppermute | solution.py:245
  9.1 2.0 %edge_lines.1 = (f32[16,2560]{1,0:T(8,128)}, f32[16,2560]{1,0:T(8,128)}, f32[16,2560]{1,0:T(8,128)}, f32[16,2560]{1,0:T(8,128)}) custom-call(f32[8,16,2560]{2,1,0:T(8,128)} %copy_bitcast_fusion.packed_ref), custom_call_target="tpu_custom_call" | custom-call | tf_op jit(solution)/shard_map/edge_lines/pallas_call | solution.py:249
  11.1 0.7 %collective-permute-start.2 = (f32[16,2560]{1,0:T(8,128)}, f32[16,2560]{1,0:T(8,128)S(1)}, u32[]{:S(2)}, u32[]{:S(2)}) collective-permute-start(f32[16,2560]{1,0:T(8,128)} %get-tuple-element.6), channel_id=1, source_target_pairs={{8,4},{4,8},{9,5},{5,9},{10,6},{6,10},{11,7},{7,11},{24,20},{20,24... | collective-permute-start | bytes 491528 | tf_op jit(solution)/shard_map/ppermute | solution.py:274
  11.8 0.7 %collective-permute-start.3 = (f32[16,2560]{1,0:T(8,128)}, f32[16,2560]{1,0:T(8,128)S(1)}, u32[]{:S(2)}, u32[]{:S(2)}) collective-permute-start(f32[16,2560]{1,0:T(8,128)} %get-tuple-element.7), channel_id=1, source_target_pairs={{8,5},{4,9},{9,4},{5,8},{10,7},{6,11},{11,6},{7,10},{24,21},{20,25... | collective-permute-start | bytes 491528 | tf_op jit(solution)/shard_map/ppermute | solution.py:274
  12.5 0.7 %collective-permute-start.4 = (f32[16,2560]{1,0:T(8,128)}, f32[16,2560]{1,0:T(8,128)S(1)}, u32[]{:S(2)}, u32[]{:S(2)}) collective-permute-start(f32[16,2560]{1,0:T(8,128)} %get-tuple-element.8), channel_id=1, source_target_pairs={{8,6},{4,10},{9,7},{5,11},{10,4},{6,8},{11,5},{7,9},{24,22},{20,26... | collective-permute-start | bytes 491528 | tf_op jit(solution)/shard_map/ppermute | solution.py:274
  13.2 0.7 %collective-permute-start.5 = (f32[16,2560]{1,0:T(8,128)}, f32[16,2560]{1,0:T(8,128)S(1)}, u32[]{:S(2)}, u32[]{:S(2)}) collective-permute-start(f32[16,2560]{1,0:T(8,128)} %get-tuple-element.9), channel_id=1, source_target_pairs={{8,7},{4,11},{9,6},{5,10},{10,5},{6,9},{11,4},{7,8},{24,23},{20,27... | collective-permute-start | bytes 491528 | tf_op jit(solution)/shard_map/ppermute | solution.py:274
  13.9 0.0 copy-done.4
  13.9 0.1 dynamic_slice.7
  14.0 0.1 dynamic_slice.6
  14.0 0.0 copy-done.2
  14.0 0.2 convert_reduce_fusion
  14.2 0.0 copy-done.3
  14.2 0.1 maximum_multiply_fusion
  14.3 0.0 collective-permute-done
  14.4 0.7 %collective-permute-start.1 = (f32[8,2560]{1,0:T(8,128)S(1)}, f32[8,2560]{1,0:T(8,128)S(1)}, u32[]{:S(2)}, u32[]{:S(2)}) collective-permute-start(f32[8,2560]{1,0:T(8,128)S(1)} %maximum_select_fusion), channel_id=1, source_target_pairs={{0,0},{1,8},{2,1},{3,9},{4,2},{5,10},{6,3},{7,11},{8,4},{9,12},{10... | collective-permute-start | bytes 245768 | tf_op jit(solution)/shard_map/ppermute | solution.py:284
  15.0 0.1 pad_add_fusion.place_ref
  15.1 0.0 collective-permute-done.1.phase_ref
  15.1 0.0 collective-permute-done.2
  15.1 0.0 collective-permute-done.3
  15.1 0.0 collective-permute-done.4
  15.1 0.0 collective-permute-done.5
  15.2 10.6 %all-to-all-done = f32[8,16,2560]{2,1,0:T(8,128)S(1)} async-done(((f32[8,16,2560]{2,1,0:T(8,128)}), f32[8,16,2560]{2,1,0:T(8,128)S(1)}, u32[]{:S(2)}, u32[]{:S(2)}) %all-to-all-start) | async-done | bytes 1310752 | tf_op jit(solution)/shard_map/all_to_all | solution.py:258
  25.8 0.1 broadcast_in_dim.16.factor_ref
  25.9 4.2 %pair_products.1 = f32[384,128]{1,0:T(8,128)S(1)} custom-call(s32[66]{0:T(128)S(1)} %pad_add_fusion.place_ref, f32[16,128]{1,0:T(8,128)S(1)} %broadcast_in_dim.16.factor_ref, f32[8,2560]{1,0:T(8,128)S(1)} %collective-permute-done.1.phase_ref, f32[2560,128]{1,0:T(8,128)S(1)} %bitcast.52, f32[320,128]{1,0:T(8,128)S(1)} %bitcast.55, f32[320,128]{1,0:T(8,128)S(1)} %bitcast.56, ...), custom_call_target="tpu_custom_call" | custom-call | tf_op jit(solution)/shard_map/pair_products/pallas_call | solution.py:302
  30.1 20.7 %all_to_all.10 = f32[16,24,128]{2,1,0:T(8,128)S(1)} all-to-all(f32[16,24,128]{2,1,0:T(8,128)S(1)} %bitcast.53), channel_id=1, replica_groups=mesh['groups'=2,'date'=16] {'date'}, dimensions={0} | all-to-all | bytes 393216 | tf_op jit(solution)/shard_map/all_to_all | solution.py:322
  50.7 0.7 %collect_slots.1 = (f32[4,2,16,128]{3,2,1,0:T(8,128)}, f32[4,16,128]{2,1,0:T(8,128)}) custom-call(f32[384,128]{1,0:T(8,128)S(1)} %bitcast.54), custom_call_target="tpu_custom_call" | custom-call | tf_op jit(solution)/shard_map/collect_slots/pallas_call | solution.py:330
  (3 shorter events, 0.0 us)
Async XLA Ops:
  0.6 1.3 %copy-start = (f32[1,2,64,2560]{3,2,1,0:T(8,128)S(1)}, f32[1,2,64,2560]{3,2,1,0:T(8,128)}, u32[]{:S(2)}) copy-start(f32[1,2,64,2560]{3,2,1,0:T(8,128)} %param.5) | copy-start | bytes 3932164
  3.1 5.4 %copy-start.1 = (f32[4,2560]{1,0:T(4,128)S(1)}, f32[4,2560]{1,0:T(4,128)}, u32[]{:S(2)}) copy-start(f32[4,2560]{1,0:T(4,128)} %param.6) | copy-start | bytes 122884
  3.1 22.7 %all-to-all-start = ((f32[8,16,2560]{2,1,0:T(8,128)}), f32[8,16,2560]{2,1,0:T(8,128)S(1)}, u32[]{:S(2)}, u32[]{:S(2)}) async-start(f32[8,16,2560]{2,1,0:T(8,128)} %copy_bitcast_fusion.packed_ref), calls=%async_computation | async-start | bytes 2621440 | tf_op jit(solution)/shard_map/all_to_all | solution.py:258
  8.5 5.4 %copy-start.4 = (f32[16]{0:T(128)S(1)}, f32[16]{0:T(128)}, u32[]{:S(2)}) copy-start(f32[16]{0:T(128)} %param.7) | copy-start | bytes 196
  8.5 5.5 %copy-start.2 = (s32[32,1]{0,1:T(1,128)S(1)}, s32[32,1]{0,1:T(1,128)}, u32[]{:S(2)}) copy-start(s32[32,1]{0,1:T(1,128)} %param.9) | copy-start | bytes 388
  8.5 5.7 %copy-start.3 = (s32[32,2]{0,1:T(2,128)S(1)}, s32[32,2]{0,1:T(2,128)}, u32[]{:S(2)}) copy-start(s32[32,2]{0,1:T(2,128)} %param.8) | copy-start | bytes 772
  8.6 5.8 %collective-permute-start = (f32[4,2560]{1,0:T(4,128)S(1)}, f32[4,2560]{1,0:T(4,128)S(1)}, u32[]{:S(2)}, u32[]{:S(2)}) collective-permute-start(f32[4,2560]{1,0:T(4,128)S(1)} %copy-done.1), channel_id=1, source_target_pairs={{0,1},{1,0},{2,3},{3,2},{4,5},{5,4},{6,7},{7,6},{8,9},{9,8},{10,11... | collective-permute-start | bytes 122888 | tf_op jit(solution)/shard_map/ppermute | solution.py:245
  11.1 4.0 %collective-permute-start.2 = (f32[16,2560]{1,0:T(8,128)}, f32[16,2560]{1,0:T(8,128)S(1)}, u32[]{:S(2)}, u32[]{:S(2)}) collective-permute-start(f32[16,2560]{1,0:T(8,128)} %get-tuple-element.6), channel_id=1, source_target_pairs={{8,4},{4,8},{9,5},{5,9},{10,6},{6,10},{11,7},{7,11},{24,20},{20,24... | collective-permute-start | bytes 491528 | tf_op jit(solution)/shard_map/ppermute | solution.py:274
  11.8 3.3 %collective-permute-start.3 = (f32[16,2560]{1,0:T(8,128)}, f32[16,2560]{1,0:T(8,128)S(1)}, u32[]{:S(2)}, u32[]{:S(2)}) collective-permute-start(f32[16,2560]{1,0:T(8,128)} %get-tuple-element.7), channel_id=1, source_target_pairs={{8,5},{4,9},{9,4},{5,8},{10,7},{6,11},{11,6},{7,10},{24,21},{20,25... | collective-permute-start | bytes 491528 | tf_op jit(solution)/shard_map/ppermute | solution.py:274
  12.5 2.6 %collective-permute-start.4 = (f32[16,2560]{1,0:T(8,128)}, f32[16,2560]{1,0:T(8,128)S(1)}, u32[]{:S(2)}, u32[]{:S(2)}) collective-permute-start(f32[16,2560]{1,0:T(8,128)} %get-tuple-element.8), channel_id=1, source_target_pairs={{8,6},{4,10},{9,7},{5,11},{10,4},{6,8},{11,5},{7,9},{24,22},{20,26... | collective-permute-start | bytes 491528 | tf_op jit(solution)/shard_map/ppermute | solution.py:274
  13.2 2.0 %collective-permute-start.5 = (f32[16,2560]{1,0:T(8,128)}, f32[16,2560]{1,0:T(8,128)S(1)}, u32[]{:S(2)}, u32[]{:S(2)}) collective-permute-start(f32[16,2560]{1,0:T(8,128)} %get-tuple-element.9), channel_id=1, source_target_pairs={{8,7},{4,11},{9,6},{5,10},{10,5},{6,9},{11,4},{7,8},{24,23},{20,27... | collective-permute-start | bytes 491528 | tf_op jit(solution)/shard_map/ppermute | solution.py:274
  14.4 0.8 %collective-permute-start.1 = (f32[8,2560]{1,0:T(8,128)S(1)}, f32[8,2560]{1,0:T(8,128)S(1)}, u32[]{:S(2)}, u32[]{:S(2)}) collective-permute-start(f32[8,2560]{1,0:T(8,128)S(1)} %maximum_select_fusion), channel_id=1, source_target_pairs={{0,0},{1,8},{2,1},{3,9},{4,2},{5,10},{6,3},{7,11},{8,4},{9,12},{10... | collective-permute-start | bytes 245768 | tf_op jit(solution)/shard_map/ppermute | solution.py:284

commit v3 on v2

--- a/solution.py
+++ b/solution.py
@@ -162,18 +162,18 @@
     def sum_row(kind, b, tile):
         return (kind * tiles * ROW_SETS + b * (1 if kind == edge_kind else tiles) + tile) * SUB
 
-    lax.fori_loop(0, blocks, block, 0)
+    lax.fori_loop(0, blocks, block, 0, unroll=4 if tiles == 1 else 1)
 
     box = box_ref[...]
     looked = None
     for part in range(sum_ref.shape[1] // box_columns):
         rest_of = sum_ref[:, part * box_columns : (part + 1) * box_columns]
         parts = None
-        for piece in range(3):
+        for piece in range(2):
             rounded = rest_of.astype(jnp.bfloat16)
             value = jnp.dot(rounded, box, preferred_element_type=jnp.float32)
             parts = value if parts is None else parts + value
-            if piece < 2:
+            if piece < 1:
                 rest_of = rest_of - rounded.astype(jnp.float32)
         if part:
             parts = pltpu.roll(parts, part * (box_columns // LOOK_COLS), 1)

time: 51.8 us -> 51.4 us (level)
  no operation moved by 1% of the time
where the time goes in v3:
time: 51.4 us; the launch traced here: 51 us
  blocking collectives  20.7 us (40%)
  waiting for transfers between devices  10.6 us (21%)
  starting transfers between devices  9.29 us (18%)
  Pallas kernels  6.49 us (13%)
  local copies, waits for them, and re-layouts  2.73 us (5%)
  between operations  0.8 us (2%)
    all_to_all x1, blocking collectives, body(): lax.all_to_all(buffer.reshape(devices, CAP * SLOT_ROWS, LANES), 'date', s...  20.7 us
    all_to_all x1, waiting for transfers between devices, body(): lax.all_to_all(packed, 'date', split_axis=0, concat_axis=0, tiled=True, a...  10.6 us
    all_to_all x1, starting transfers between devices, body(): lax.all_to_all(packed, 'date', split_axis=0, concat_axis=0, tiled=True, a...  5.39 us
    pallas_call x1, Pallas kernels, body(): pl.pallas_call(functools.partial(pair_kernel, half, blocks, pairs), out_s...  3.8 us
    ppermute x4, starting transfers between devices, body(): got = lax.ppermute(edges[BAND * g + i], 'date', steps)  2.68 us
    pallas_call x1, Pallas kernels, body(): pl.pallas_call(functools.partial(edge_kernel, half), out_shape=[jax.Shape...  2.01 us
    unnamed x10, local copies, waits for them, and re-layouts  1.34 us
    reshape x1, local copies, waits for them, and re-layouts, body(): packed = packed.reshape(half, 2 * SUB, columns)  1.17 us
  transfers between devices with their start and end apart: 7, of which 1 were waited for; matrix products, arithmetic and copies ran while one was open for 1% of the time, Pallas kernels for 4%

profile of v3, /device:TPU:0, one launch (start us, length us, event | category | flops | bytes accessed | tf_op | source)
XLA Modules:
  0.0 51.0 jit_solution(6963205713110112976)
XLA Ops:
  0.6 0.0 copy-start
  0.6 1.3 %copy-done = f32[1,2,64,2560]{3,2,1,0:T(8,128)S(1)} copy-done((f32[1,2,64,2560]{3,2,1,0:T(8,128)S(1)}, f32[1,2,64,2560]{3,2,1,0:T(8,128)}, u32[]{:S(2)}) %copy-start) | copy-done | bytes 1310744
  2.0 1.2 %copy_bitcast_fusion.packed_ref = f32[8,16,2560]{2,1,0:T(8,128)} fusion(f32[1,2,64,2560]{3,2,1,0:T(8,128)S(1)} %copy-done), kind=kLoop, calls=%fused_computation | loop fusion | bytes 2621440 | tf_op jit(solution)/shard_map/reshape | solution.py:248
  3.1 0.0 copy-start.1
  3.1 5.4 %all-to-all-start = ((f32[8,16,2560]{2,1,0:T(8,128)}), f32[8,16,2560]{2,1,0:T(8,128)S(1)}, u32[]{:S(2)}, u32[]{:S(2)}) async-start(f32[8,16,2560]{2,1,0:T(8,128)} %copy_bitcast_fusion.packed_ref), calls=%async_computation | async-start | bytes 2621440 | tf_op jit(solution)/shard_map/all_to_all | solution.py:258
  8.5 0.0 copy-done.1
  8.5 0.0 copy-start.4
  8.5 0.0 copy-start.2
  8.5 0.0 copy-start.3
  8.6 0.6 %collective-permute-start = (f32[4,2560]{1,0:T(4,128)S(1)}, f32[4,2560]{1,0:T(4,128)S(1)}, u32[]{:S(2)}, u32[]{:S(2)}) collective-permute-start(f32[4,2560]{1,0:T(4,128)S(1)} %copy-done.1), channel_id=1, source_target_pairs={{0,1},{1,0},{2,3},{3,2},{4,5},{5,4},{6,7},{7,6},{8,9},{9,8},{10,11... | collective-permute-start | bytes 122888 | tf_op jit(solution)/shard_map/ppermute | solution.py:245
  9.1 2.0 %edge_lines.1 = (f32[16,2560]{1,0:T(8,128)}, f32[16,2560]{1,0:T(8,128)}, f32[16,2560]{1,0:T(8,128)}, f32[16,2560]{1,0:T(8,128)}) custom-call(f32[8,16,2560]{2,1,0:T(8,128)} %copy_bitcast_fusion.packed_ref), custom_call_target="tpu_custom_call" | custom-call | tf_op jit(solution)/shard_map/edge_lines/pallas_call | solution.py:249
  11.1 0.7 %collective-permute-start.2 = (f32[16,2560]{1,0:T(8,128)}, f32[16,2560]{1,0:T(8,128)S(1)}, u32[]{:S(2)}, u32[]{:S(2)}) collective-permute-start(f32[16,2560]{1,0:T(8,128)} %get-tuple-element.6), channel_id=1, source_target_pairs={{8,4},{4,8},{9,5},{5,9},{10,6},{6,10},{11,7},{7,11},{24,20},{20,24... | collective-permute-start | bytes 491528 | tf_op jit(solution)/shard_map/ppermute | solution.py:274
  11.8 0.7 %collective-permute-start.3 = (f32[16,2560]{1,0:T(8,128)}, f32[16,2560]{1,0:T(8,128)S(1)}, u32[]{:S(2)}, u32[]{:S(2)}) collective-permute-start(f32[16,2560]{1,0:T(8,128)} %get-tuple-element.7), channel_id=1, source_target_pairs={{8,5},{4,9},{9,4},{5,8},{10,7},{6,11},{11,6},{7,10},{24,21},{20,25... | collective-permute-start | bytes 491528 | tf_op jit(solution)/shard_map/ppermute | solution.py:274
  12.5 0.7 %collective-permute-start.4 = (f32[16,2560]{1,0:T(8,128)}, f32[16,2560]{1,0:T(8,128)S(1)}, u32[]{:S(2)}, u32[]{:S(2)}) collective-permute-start(f32[16,2560]{1,0:T(8,128)} %get-tuple-element.8), channel_id=1, source_target_pairs={{8,6},{4,10},{9,7},{5,11},{10,4},{6,8},{11,5},{7,9},{24,22},{20,26... | collective-permute-start | bytes 491528 | tf_op jit(solution)/shard_map/ppermute | solution.py:274
  13.2 0.7 %collective-permute-start.5 = (f32[16,2560]{1,0:T(8,128)}, f32[16,2560]{1,0:T(8,128)S(1)}, u32[]{:S(2)}, u32[]{:S(2)}) collective-permute-start(f32[16,2560]{1,0:T(8,128)} %get-tuple-element.9), channel_id=1, source_target_pairs={{8,7},{4,11},{9,6},{5,10},{10,5},{6,9},{11,4},{7,8},{24,23},{20,27... | collective-permute-start | bytes 491528 | tf_op jit(solution)/shard_map/ppermute | solution.py:274
  13.9 0.0 copy-done.4
  13.9 0.1 dynamic_slice.7
  14.0 0.1 dynamic_slice.6
  14.0 0.0 copy-done.2
  14.0 0.2 convert_reduce_fusion
  14.2 0.0 copy-done.3
  14.2 0.1 maximum_multiply_fusion
  14.3 0.0 collective-permute-done
  14.4 0.7 %collective-permute-start.1 = (f32[8,2560]{1,0:T(8,128)S(1)}, f32[8,2560]{1,0:T(8,128)S(1)}, u32[]{:S(2)}, u32[]{:S(2)}) collective-permute-start(f32[8,2560]{1,0:T(8,128)S(1)} %maximum_select_fusion), channel_id=1, source_target_pairs={{0,0},{1,8},{2,1},{3,9},{4,2},{5,10},{6,3},{7,11},{8,4},{9,12},{10... | collective-permute-start | bytes 245768 | tf_op jit(solution)/shard_map/ppermute | solution.py:284
  15.0 0.1 pad_add_fusion.place_ref
  15.1 0.0 collective-permute-done.1.phase_ref
  15.1 0.0 collective-permute-done.2
  15.1 0.0 collective-permute-done.3
  15.1 0.0 collective-permute-done.4
  15.1 0.0 collective-permute-done.5
  15.2 10.6 %all-to-all-done = f32[8,16,2560]{2,1,0:T(8,128)S(1)} async-done(((f32[8,16,2560]{2,1,0:T(8,128)}), f32[8,16,2560]{2,1,0:T(8,128)S(1)}, u32[]{:S(2)}, u32[]{:S(2)}) %all-to-all-start) | async-done | bytes 1310752 | tf_op jit(solution)/shard_map/all_to_all | solution.py:258
  25.8 0.1 broadcast_in_dim.16.factor_ref
  25.9 3.8 %pair_products.1 = f32[384,128]{1,0:T(8,128)S(1)} custom-call(s32[66]{0:T(128)S(1)} %pad_add_fusion.place_ref, f32[16,128]{1,0:T(8,128)S(1)} %broadcast_in_dim.16.factor_ref, f32[8,2560]{1,0:T(8,128)S(1)} %collective-permute-done.1.phase_ref, f32[2560,128]{1,0:T(8,128)S(1)} %bitcast.52, f32[320,128]{1,0:T(8,128)S(1)} %bitcast.55, f32[320,128]{1,0:T(8,128)S(1)} %bitcast.56, ...), custom_call_target="tpu_custom_call" | custom-call | tf_op jit(solution)/shard_map/pair_products/pallas_call | solution.py:302
  29.7 20.7 %all_to_all.10 = f32[16,24,128]{2,1,0:T(8,128)S(1)} all-to-all(f32[16,24,128]{2,1,0:T(8,128)S(1)} %bitcast.53), channel_id=1, replica_groups=mesh['groups'=2,'date'=16] {'date'}, dimensions={0} | all-to-all | bytes 393216 | tf_op jit(solution)/shard_map/all_to_all | solution.py:322
  50.3 0.7 %collect_slots.1 = (f32[4,2,16,128]{3,2,1,0:T(8,128)}, f32[4,16,128]{2,1,0:T(8,128)}) custom-call(f32[384,128]{1,0:T(8,128)S(1)} %bitcast.54), custom_call_target="tpu_custom_call" | custom-call | tf_op jit(solution)/shard_map/collect_slots/pallas_call | solution.py:330
  (3 shorter events, 0.0 us)
Async XLA Ops:
  0.6 1.3 %copy-start = (f32[1,2,64,2560]{3,2,1,0:T(8,128)S(1)}, f32[1,2,64,2560]{3,2,1,0:T(8,128)}, u32[]{:S(2)}) copy-start(f32[1,2,64,2560]{3,2,1,0:T(8,128)} %param.5) | copy-start | bytes 3932164
  3.1 5.4 %copy-start.1 = (f32[4,2560]{1,0:T(4,128)S(1)}, f32[4,2560]{1,0:T(4,128)}, u32[]{:S(2)}) copy-start(f32[4,2560]{1,0:T(4,128)} %param.6) | copy-start | bytes 122884
  3.1 22.7 %all-to-all-start = ((f32[8,16,2560]{2,1,0:T(8,128)}), f32[8,16,2560]{2,1,0:T(8,128)S(1)}, u32[]{:S(2)}, u32[]{:S(2)}) async-start(f32[8,16,2560]{2,1,0:T(8,128)} %copy_bitcast_fusion.packed_ref), calls=%async_computation | async-start | bytes 2621440 | tf_op jit(solution)/shard_map/all_to_all | solution.py:258
  8.5 5.4 %copy-start.4 = (f32[16]{0:T(128)S(1)}, f32[16]{0:T(128)}, u32[]{:S(2)}) copy-start(f32[16]{0:T(128)} %param.7) | copy-start | bytes 196
  8.5 5.5 %copy-start.2 = (s32[32,1]{0,1:T(1,128)S(1)}, s32[32,1]{0,1:T(1,128)}, u32[]{:S(2)}) copy-start(s32[32,1]{0,1:T(1,128)} %param.9) | copy-start | bytes 388
  8.5 5.7 %copy-start.3 = (s32[32,2]{0,1:T(2,128)S(1)}, s32[32,2]{0,1:T(2,128)}, u32[]{:S(2)}) copy-start(s32[32,2]{0,1:T(2,128)} %param.8) | copy-start | bytes 772
  8.6 5.8 %collective-permute-start = (f32[4,2560]{1,0:T(4,128)S(1)}, f32[4,2560]{1,0:T(4,128)S(1)}, u32[]{:S(2)}, u32[]{:S(2)}) collective-permute-start(f32[4,2560]{1,0:T(4,128)S(1)} %copy-done.1), channel_id=1, source_target_pairs={{0,1},{1,0},{2,3},{3,2},{4,5},{5,4},{6,7},{7,6},{8,9},{9,8},{10,11... | collective-permute-start | bytes 122888 | tf_op jit(solution)/shard_map/ppermute | solution.py:245
  11.1 4.0 %collective-permute-start.2 = (f32[16,2560]{1,0:T(8,128)}, f32[16,2560]{1,0:T(8,128)S(1)}, u32[]{:S(2)}, u32[]{:S(2)}) collective-permute-start(f32[16,2560]{1,0:T(8,128)} %get-tuple-element.6), channel_id=1, source_target_pairs={{8,4},{4,8},{9,5},{5,9},{10,6},{6,10},{11,7},{7,11},{24,20},{20,24... | collective-permute-start | bytes 491528 | tf_op jit(solution)/shard_map/ppermute | solution.py:274
  11.8 3.3 %collective-permute-start.3 = (f32[16,2560]{1,0:T(8,128)}, f32[16,2560]{1,0:T(8,128)S(1)}, u32[]{:S(2)}, u32[]{:S(2)}) collective-permute-start(f32[16,2560]{1,0:T(8,128)} %get-tuple-element.7), channel_id=1, source_target_pairs={{8,5},{4,9},{9,4},{5,8},{10,7},{6,11},{11,6},{7,10},{24,21},{20,25... | collective-permute-start | bytes 491528 | tf_op jit(solution)/shard_map/ppermute | solution.py:274
  12.5 2.6 %collective-permute-start.4 = (f32[16,2560]{1,0:T(8,128)}, f32[16,2560]{1,0:T(8,128)S(1)}, u32[]{:S(2)}, u32[]{:S(2)}) collective-permute-start(f32[16,2560]{1,0:T(8,128)} %get-tuple-element.8), channel_id=1, source_target_pairs={{8,6},{4,10},{9,7},{5,11},{10,4},{6,8},{11,5},{7,9},{24,22},{20,26... | collective-permute-start | bytes 491528 | tf_op jit(solution)/shard_map/ppermute | solution.py:274
  13.2 2.0 %collective-permute-start.5 = (f32[16,2560]{1,0:T(8,128)}, f32[16,2560]{1,0:T(8,128)S(1)}, u32[]{:S(2)}, u32[]{:S(2)}) collective-permute-start(f32[16,2560]{1,0:T(8,128)} %get-tuple-element.9), channel_id=1, source_target_pairs={{8,7},{4,11},{9,6},{5,10},{10,5},{6,9},{11,4},{7,8},{24,23},{20,27... | collective-permute-start | bytes 491528 | tf_op jit(solution)/shard_map/ppermute | solution.py:274
  14.4 0.8 %collective-permute-start.1 = (f32[8,2560]{1,0:T(8,128)S(1)}, f32[8,2560]{1,0:T(8,128)S(1)}, u32[]{:S(2)}, u32[]{:S(2)}) collective-permute-start(f32[8,2560]{1,0:T(8,128)S(1)} %maximum_select_fusion), channel_id=1, source_target_pairs={{0,0},{1,8},{2,1},{3,9},{4,2},{5,10},{6,3},{7,11},{8,4},{9,12},{10... | collective-permute-start | bytes 245768 | tf_op jit(solution)/shard_map/ppermute | solution.py:284

commit v4 on v3

--- a/solution.py
+++ b/solution.py
@@ -105,8 +105,11 @@
     edge_kind = 1 + 2 * BAND
 
     def block(t, carry):
-        line_at = pl.multiple_of(t * SUB, SUB)
-        column = pl.ds(pl.multiple_of(t * LANES, LANES), LANES)
+        line_at = t * SUB
+        column = pl.ds(t * LANES, LANES)
+        if not isinstance(t, int):
+            line_at = pl.multiple_of(line_at, SUB)
+            column = pl.ds(pl.multiple_of(t * LANES, LANES), LANES)
         for part in range(2):
             for i in range(BAND):
                 row = jnp.bitwise_xor(lane, i)
@@ -162,11 +165,16 @@
     def sum_row(kind, b, tile):
         return (kind * tiles * ROW_SETS + b * (1 if kind == edge_kind else tiles) + tile) * SUB
 
-    lax.fori_loop(0, blocks, block, 0, unroll=4 if tiles == 1 else 1)
-
     box = box_ref[...]
     looked = None
-    for part in range(sum_ref.shape[1] // box_columns):
+    for part in range(BOX_PARTS):
+        first = part * (blocks // BOX_PARTS)
+        last = first + blocks // BOX_PARTS
+        if tiles == 1:
+            for t in range(first, last):
+                block(t, 0)
+        else:
+            lax.fori_loop(first, last, block, 0)
         rest_of = sum_ref[:, part * box_columns : (part + 1) * box_columns]
         parts = None
         for piece in range(2):

time: 51.4 us -> 51.5 us (level)
  no operation moved by 1% of the time
where the time goes in v4:
time: 51.5 us; the launch traced here: 51 us
  blocking collectives  20.7 us (40%)
  waiting for transfers between devices  10.6 us (21%)
  starting transfers between devices  9.29 us (18%)
  Pallas kernels  6.53 us (13%)
  local copies, waits for them, and re-layouts  2.73 us (5%)
  between operations  0.8 us (2%)
    all_to_all x1, blocking collectives, body(): lax.all_to_all(buffer.reshape(devices, CAP * SLOT_ROWS, LANES), 'date', s...  20.7 us
    all_to_all x1, waiting for transfers between devices, body(): lax.all_to_all(packed, 'date', split_axis=0, concat_axis=0, tiled=True, a...  10.6 us
    all_to_all x1, starting transfers between devices, body(): lax.all_to_all(packed, 'date', split_axis=0, concat_axis=0, tiled=True, a...  5.39 us
    pallas_call x1, Pallas kernels, body(): pl.pallas_call(functools.partial(pair_kernel, half, blocks, pairs), out_s...  3.85 us
    ppermute x4, starting transfers between devices, body(): got = lax.ppermute(edges[BAND * g + i], 'date', steps)  2.68 us
    pallas_call x1, Pallas kernels, body(): pl.pallas_call(functools.partial(edge_kernel, half), out_shape=[jax.Shape...  2.01 us
    unnamed x10, local copies, waits for them, and re-layouts  1.34 us
    reshape x1, local copies, waits for them, and re-layouts, body(): packed = packed.reshape(half, 2 * SUB, columns)  1.17 us
  transfers between devices with their start and end apart: 7, of which 1 were waited for; matrix products, arithmetic and copies ran while one was open for 1% of the time, Pallas kernels for 4%

profile of v4, /device:TPU:0, one launch (start us, length us, event | category | flops | bytes accessed | tf_op | source)
XLA Modules:
  0.0 51.0 jit_solution(2053759435503031667)
XLA Ops:
  0.6 0.0 copy-start
  0.6 1.3 %copy-done = f32[1,2,64,2560]{3,2,1,0:T(8,128)S(1)} copy-done((f32[1,2,64,2560]{3,2,1,0:T(8,128)S(1)}, f32[1,2,64,2560]{3,2,1,0:T(8,128)}, u32[]{:S(2)}) %copy-start) | copy-done | bytes 1310744
  2.0 1.2 %copy_bitcast_fusion.packed_ref = f32[8,16,2560]{2,1,0:T(8,128)} fusion(f32[1,2,64,2560]{3,2,1,0:T(8,128)S(1)} %copy-done), kind=kLoop, calls=%fused_computation | loop fusion | bytes 2621440 | tf_op jit(solution)/shard_map/reshape | solution.py:256
  3.1 0.0 copy-start.1
  3.1 5.4 %all-to-all-start = ((f32[8,16,2560]{2,1,0:T(8,128)}), f32[8,16,2560]{2,1,0:T(8,128)S(1)}, u32[]{:S(2)}, u32[]{:S(2)}) async-start(f32[8,16,2560]{2,1,0:T(8,128)} %copy_bitcast_fusion.packed_ref), calls=%async_computation | async-start | bytes 2621440 | tf_op jit(solution)/shard_map/all_to_all | solution.py:266
  8.5 0.0 copy-done.1
  8.5 0.0 copy-start.4
  8.5 0.0 copy-start.2
  8.5 0.0 copy-start.3
  8.6 0.6 %collective-permute-start = (f32[4,2560]{1,0:T(4,128)S(1)}, f32[4,2560]{1,0:T(4,128)S(1)}, u32[]{:S(2)}, u32[]{:S(2)}) collective-permute-start(f32[4,2560]{1,0:T(4,128)S(1)} %copy-done.1), channel_id=1, source_target_pairs={{0,1},{1,0},{2,3},{3,2},{4,5},{5,4},{6,7},{7,6},{8,9},{9,8},{10,11... | collective-permute-start | bytes 122888 | tf_op jit(solution)/shard_map/ppermute | solution.py:253
  9.1 2.0 %edge_lines.1 = (f32[16,2560]{1,0:T(8,128)}, f32[16,2560]{1,0:T(8,128)}, f32[16,2560]{1,0:T(8,128)}, f32[16,2560]{1,0:T(8,128)}) custom-call(f32[8,16,2560]{2,1,0:T(8,128)} %copy_bitcast_fusion.packed_ref), custom_call_target="tpu_custom_call" | custom-call | tf_op jit(solution)/shard_map/edge_lines/pallas_call | solution.py:257
  11.1 0.7 %collective-permute-start.2 = (f32[16,2560]{1,0:T(8,128)}, f32[16,2560]{1,0:T(8,128)S(1)}, u32[]{:S(2)}, u32[]{:S(2)}) collective-permute-start(f32[16,2560]{1,0:T(8,128)} %get-tuple-element.6), channel_id=1, source_target_pairs={{8,4},{4,8},{9,5},{5,9},{10,6},{6,10},{11,7},{7,11},{24,20},{20,24... | collective-permute-start | bytes 491528 | tf_op jit(solution)/shard_map/ppermute | solution.py:282
  11.8 0.7 %collective-permute-start.3 = (f32[16,2560]{1,0:T(8,128)}, f32[16,2560]{1,0:T(8,128)S(1)}, u32[]{:S(2)}, u32[]{:S(2)}) collective-permute-start(f32[16,2560]{1,0:T(8,128)} %get-tuple-element.7), channel_id=1, source_target_pairs={{8,5},{4,9},{9,4},{5,8},{10,7},{6,11},{11,6},{7,10},{24,21},{20,25... | collective-permute-start | bytes 491528 | tf_op jit(solution)/shard_map/ppermute | solution.py:282
  12.5 0.7 %collective-permute-start.4 = (f32[16,2560]{1,0:T(8,128)}, f32[16,2560]{1,0:T(8,128)S(1)}, u32[]{:S(2)}, u32[]{:S(2)}) collective-permute-start(f32[16,2560]{1,0:T(8,128)} %get-tuple-element.8), channel_id=1, source_target_pairs={{8,6},{4,10},{9,7},{5,11},{10,4},{6,8},{11,5},{7,9},{24,22},{20,26... | collective-permute-start | bytes 491528 | tf_op jit(solution)/shard_map/ppermute | solution.py:282
  13.2 0.7 %collective-permute-start.5 = (f32[16,2560]{1,0:T(8,128)}, f32[16,2560]{1,0:T(8,128)S(1)}, u32[]{:S(2)}, u32[]{:S(2)}) collective-permute-start(f32[16,2560]{1,0:T(8,128)} %get-tuple-element.9), channel_id=1, source_target_pairs={{8,7},{4,11},{9,6},{5,10},{10,5},{6,9},{11,4},{7,8},{24,23},{20,27... | collective-permute-start | bytes 491528 | tf_op jit(solution)/shard_map/ppermute | solution.py:282
  13.9 0.0 copy-done.4
  13.9 0.1 dynamic_slice.7
  14.0 0.1 dynamic_slice.6
  14.0 0.0 copy-done.2
  14.0 0.2 convert_reduce_fusion
  14.2 0.0 copy-done.3
  14.2 0.1 maximum_multiply_fusion
  14.3 0.0 collective-permute-done
  14.4 0.7 %collective-permute-start.1 = (f32[8,2560]{1,0:T(8,128)S(1)}, f32[8,2560]{1,0:T(8,128)S(1)}, u32[]{:S(2)}, u32[]{:S(2)}) collective-permute-start(f32[8,2560]{1,0:T(8,128)S(1)} %maximum_select_fusion), channel_id=1, source_target_pairs={{0,0},{1,8},{2,1},{3,9},{4,2},{5,10},{6,3},{7,11},{8,4},{9,12},{10... | collective-permute-start | bytes 245768 | tf_op jit(solution)/shard_map/ppermute | solution.py:292
  15.0 0.1 pad_add_fusion.place_ref
  15.1 0.0 collective-permute-done.1.phase_ref
  15.1 0.0 collective-permute-done.2
  15.1 0.0 collective-permute-done.3
  15.1 0.0 collective-permute-done.4
  15.1 0.0 collective-permute-done.5
  15.2 10.6 %all-to-all-done = f32[8,16,2560]{2,1,0:T(8,128)S(1)} async-done(((f32[8,16,2560]{2,1,0:T(8,128)}), f32[8,16,2560]{2,1,0:T(8,128)S(1)}, u32[]{:S(2)}, u32[]{:S(2)}) %all-to-all-start) | async-done | bytes 1310752 | tf_op jit(solution)/shard_map/all_to_all | solution.py:266
  25.8 0.1 broadcast_in_dim.16.factor_ref
  25.9 3.9 %pair_products.1 = f32[384,128]{1,0:T(8,128)S(1)} custom-call(s32[66]{0:T(128)S(1)} %pad_add_fusion.place_ref, f32[16,128]{1,0:T(8,128)S(1)} %broadcast_in_dim.16.factor_ref, f32[8,2560]{1,0:T(8,128)S(1)} %collective-permute-done.1.phase_ref, f32[2560,128]{1,0:T(8,128)S(1)} %bitcast.52, f32[320,128]{1,0:T(8,128)S(1)} %bitcast.55, f32[320,128]{1,0:T(8,128)S(1)} %bitcast.56, ...), custom_call_target="tpu_custom_call" | custom-call | tf_op jit(solution)/shard_map/pair_products/pallas_call | solution.py:310
  29.7 20.7 %all_to_all.10 = f32[16,24,128]{2,1,0:T(8,128)S(1)} all-to-all(f32[16,24,128]{2,1,0:T(8,128)S(1)} %bitcast.53), channel_id=1, replica_groups=mesh['groups'=2,'date'=16] {'date'}, dimensions={0} | all-to-all | bytes 393216 | tf_op jit(solution)/shard_map/all_to_all | solution.py:330
  50.4 0.7 %collect_slots.1 = (f32[4,2,16,128]{3,2,1,0:T(8,128)}, f32[4,16,128]{2,1,0:T(8,128)}) custom-call(f32[384,128]{1,0:T(8,128)S(1)} %bitcast.54), custom_call_target="tpu_custom_call" | custom-call | tf_op jit(solution)/shard_map/collect_slots/pallas_call | solution.py:338
  (3 shorter events, 0.0 us)
Async XLA Ops:
  0.6 1.3 %copy-start = (f32[1,2,64,2560]{3,2,1,0:T(8,128)S(1)}, f32[1,2,64,2560]{3,2,1,0:T(8,128)}, u32[]{:S(2)}) copy-start(f32[1,2,64,2560]{3,2,1,0:T(8,128)} %param.5) | copy-start | bytes 3932164
  3.1 5.4 %copy-start.1 = (f32[4,2560]{1,0:T(4,128)S(1)}, f32[4,2560]{1,0:T(4,128)}, u32[]{:S(2)}) copy-start(f32[4,2560]{1,0:T(4,128)} %param.6) | copy-start | bytes 122884
  3.1 22.7 %all-to-all-start = ((f32[8,16,2560]{2,1,0:T(8,128)}), f32[8,16,2560]{2,1,0:T(8,128)S(1)}, u32[]{:S(2)}, u32[]{:S(2)}) async-start(f32[8,16,2560]{2,1,0:T(8,128)} %copy_bitcast_fusion.packed_ref), calls=%async_computation | async-start | bytes 2621440 | tf_op jit(solution)/shard_map/all_to_all | solution.py:266
  8.5 5.4 %copy-start.4 = (f32[16]{0:T(128)S(1)}, f32[16]{0:T(128)}, u32[]{:S(2)}) copy-start(f32[16]{0:T(128)} %param.7) | copy-start | bytes 196
  8.5 5.5 %copy-start.2 = (s32[32,1]{0,1:T(1,128)S(1)}, s32[32,1]{0,1:T(1,128)}, u32[]{:S(2)}) copy-start(s32[32,1]{0,1:T(1,128)} %param.9) | copy-start | bytes 388
  8.5 5.7 %copy-start.3 = (s32[32,2]{0,1:T(2,128)S(1)}, s32[32,2]{0,1:T(2,128)}, u32[]{:S(2)}) copy-start(s32[32,2]{0,1:T(2,128)} %param.8) | copy-start | bytes 772
  8.6 5.8 %collective-permute-start = (f32[4,2560]{1,0:T(4,128)S(1)}, f32[4,2560]{1,0:T(4,128)S(1)}, u32[]{:S(2)}, u32[]{:S(2)}) collective-permute-start(f32[4,2560]{1,0:T(4,128)S(1)} %copy-done.1), channel_id=1, source_target_pairs={{0,1},{1,0},{2,3},{3,2},{4,5},{5,4},{6,7},{7,6},{8,9},{9,8},{10,11... | collective-permute-start | bytes 122888 | tf_op jit(solution)/shard_map/ppermute | solution.py:253
  11.1 4.0 %collective-permute-start.2 = (f32[16,2560]{1,0:T(8,128)}, f32[16,2560]{1,0:T(8,128)S(1)}, u32[]{:S(2)}, u32[]{:S(2)}) collective-permute-start(f32[16,2560]{1,0:T(8,128)} %get-tuple-element.6), channel_id=1, source_target_pairs={{8,4},{4,8},{9,5},{5,9},{10,6},{6,10},{11,7},{7,11},{24,20},{20,24... | collective-permute-start | bytes 491528 | tf_op jit(solution)/shard_map/ppermute | solution.py:282
  11.8 3.3 %collective-permute-start.3 = (f32[16,2560]{1,0:T(8,128)}, f32[16,2560]{1,0:T(8,128)S(1)}, u32[]{:S(2)}, u32[]{:S(2)}) collective-permute-start(f32[16,2560]{1,0:T(8,128)} %get-tuple-element.7), channel_id=1, source_target_pairs={{8,5},{4,9},{9,4},{5,8},{10,7},{6,11},{11,6},{7,10},{24,21},{20,25... | collective-permute-start | bytes 491528 | tf_op jit(solution)/shard_map/ppermute | solution.py:282
  12.5 2.6 %collective-permute-start.4 = (f32[16,2560]{1,0:T(8,128)}, f32[16,2560]{1,0:T(8,128)S(1)}, u32[]{:S(2)}, u32[]{:S(2)}) collective-permute-start(f32[16,2560]{1,0:T(8,128)} %get-tuple-element.8), channel_id=1, source_target_pairs={{8,6},{4,10},{9,7},{5,11},{10,4},{6,8},{11,5},{7,9},{24,22},{20,26... | collective-permute-start | bytes 491528 | tf_op jit(solution)/shard_map/ppermute | solution.py:282
  13.2 2.0 %collective-permute-start.5 = (f32[16,2560]{1,0:T(8,128)}, f32[16,2560]{1,0:T(8,128)S(1)}, u32[]{:S(2)}, u32[]{:S(2)}) collective-permute-start(f32[16,2560]{1,0:T(8,128)} %get-tuple-element.9), channel_id=1, source_target_pairs={{8,7},{4,11},{9,6},{5,10},{10,5},{6,9},{11,4},{7,8},{24,23},{20,27... | collective-permute-start | bytes 491528 | tf_op jit(solution)/shard_map/ppermute | solution.py:282
  14.4 0.8 %collective-permute-start.1 = (f32[8,2560]{1,0:T(8,128)S(1)}, f32[8,2560]{1,0:T(8,128)S(1)}, u32[]{:S(2)}, u32[]{:S(2)}) collective-permute-start(f32[8,2560]{1,0:T(8,128)S(1)} %maximum_select_fusion), channel_id=1, source_target_pairs={{0,0},{1,8},{2,1},{3,9},{4,2},{5,10},{6,3},{7,11},{8,4},{9,12},{10... | collective-permute-start | bytes 245768 | tf_op jit(solution)/shard_map/ppermute | solution.py:292

commit v5 on v3

--- a/solution.py
+++ b/solution.py
@@ -39,21 +39,13 @@
     return 1.0 - twice * s, twice * c
 
 
-def edge_kernel(half, packed_ref, *rest):
-    edge_refs = rest[: half // 2]
-    sem = rest[half // 2]
+def edge_kernel(half, n, packed_ref, edge_ref, sem):
     me = lax.axis_index("date")
-    lane = lax.rem(me, BAND)
     first = jnp.where(me < half, 0, half // 2)
-    arriving = []
-    for n, edge_ref in enumerate(edge_refs):
-        target = first + n // BAND * BAND + jnp.bitwise_xor(lane, n % BAND)
-        arriving.append(
-            pltpu.make_async_copy(packed_ref.at[target], edge_ref, sem.at[n])
-        )
-        arriving[-1].start()
-    for copy in arriving:
-        copy.wait()
+    target = first + n // BAND * BAND + jnp.bitwise_xor(lax.rem(me, BAND), n % BAND)
+    copy = pltpu.make_async_copy(packed_ref.at[target], edge_ref, sem)
+    copy.start()
+    copy.wait()
 
 
 def pair_kernel(half, blocks, pairs, place_ref, factor_ref, phase_ref, own_ref, *rest):
@@ -246,14 +238,17 @@
 
     packed = jnp.swapaxes(images[0].reshape(2, half, SUB, columns), 0, 1)
     packed = packed.reshape(half, 2 * SUB, columns)
-    edges = pl.pallas_call(
-        functools.partial(edge_kernel, half),
-        out_shape=[jax.ShapeDtypeStruct((2 * SUB, columns), jnp.float32)] * (half // 2),
-        in_specs=[pl.BlockSpec(memory_space=pltpu.HBM)],
-        out_specs=[vmem] * (half // 2),
-        scratch_shapes=[pltpu.SemaphoreType.DMA((half // 2,))],
-        name="edge_lines",
-    )(packed)
+    edges = [
+        pl.pallas_call(
+            functools.partial(edge_kernel, half, n),
+            out_shape=jax.ShapeDtypeStruct((2 * SUB, columns), jnp.float32),
+            in_specs=[pl.BlockSpec(memory_space=pltpu.HBM)],
+            out_specs=vmem,
+            scratch_shapes=[pltpu.SemaphoreType.DMA],
+            name="edge_lines",
+        )(packed)
+        for n in range(half // 2)
+    ]
     halves = [list(range(half)), list(range(half, devices))]
     own = lax.all_to_all(
         packed, "date", split_axis=0, concat_axis=0, tiled=True, axis_index_groups=halves

time: 51.4 us -> 54.4 us (1.058)
  waiting for transfers between devices: 10.6 us -> 6.2 us
  Pallas kernels: 6.49 us -> 10.8 us
  blocking collectives: 20.7 us -> 23.6 us
    all_to_all x1, waiting for transfers between devices: 10.6 us -> 6.19 us  [body(): lax.all_to_all(packed, 'date', split_axis=0, concat_axis=0, tiled=True, a...]
    pallas_call x1 -> x4, Pallas kernels: 2.01 us -> 6.35 us  [body(): pl.pallas_call(functools.partial(edge_kernel, half, n), out_shape=jax.Sha...]
    all_to_all x1, blocking collectives: 20.7 us -> 23.6 us  [body(): lax.all_to_all(buffer.reshape(devices, CAP * SLOT_ROWS, LANES), 'date', s...]
  transfers between devices with their start and end apart: 7 -> 7, of which waited for: 1 -> 1; matrix products, arithmetic and copies ran while one was open for 1% -> 1% of each run, Pallas kernels for 4% -> 12%
where the time goes in v5:
time: 54.4 us; the launch traced here: 53.9 us
  blocking collectives  23.6 us (43%)
  Pallas kernels  10.8 us (20%)
  starting transfers between devices  9.37 us (17%)
  waiting for transfers between devices  6.2 us (11%)
  local copies, waits for them, and re-layouts  2.74 us (5%)
  between operations  0.83 us (2%)
    all_to_all x1, blocking collectives, body(): lax.all_to_all(buffer.reshape(devices, CAP * SLOT_ROWS, LANES), 'date', s...  23.6 us
    pallas_call x4, Pallas kernels, body(): pl.pallas_call(functools.partial(edge_kernel, half, n), out_shape=jax.Sha...  6.35 us
    all_to_all x1, waiting for transfers between devices, body(): lax.all_to_all(packed, 'date', split_axis=0, concat_axis=0, tiled=True, a...  6.19 us
    all_to_all x1, starting transfers between devices, body(): lax.all_to_all(packed, 'date', split_axis=0, concat_axis=0, tiled=True, a...  5.39 us
    pallas_call x1, Pallas kernels, body(): pl.pallas_call(functools.partial(pair_kernel, half, blocks, pairs), out_s...  3.8 us
    ppermute x4, starting transfers between devices, body(): got = lax.ppermute(edges[BAND * g + i], 'date', steps)  2.82 us
    unnamed x10, local copies, waits for them, and re-layouts  1.34 us
    reshape x1, local copies, waits for them, and re-layouts, body(): packed = packed.reshape(half, 2 * SUB, columns)  1.18 us
  transfers between devices with their start and end apart: 7, of which 1 were waited for; matrix products, arithmetic and copies ran while one was open for 1% of the time, Pallas kernels for 12%

profile of v5, /device:TPU:0, one launch (start us, length us, event | category | flops | bytes accessed | tf_op | source)
XLA Modules:
  0.0 53.9 jit_solution(10006611296219983348)
XLA Ops:
  0.6 0.0 copy-start
  0.6 1.3 %copy-done = f32[1,2,64,2560]{3,2,1,0:T(8,128)S(1)} copy-done((f32[1,2,64,2560]{3,2,1,0:T(8,128)S(1)}, f32[1,2,64,2560]{3,2,1,0:T(8,128)}, u32[]{:S(2)}) %copy-start) | copy-done | bytes 1310744
  2.0 1.2 %copy_bitcast_fusion.packed_ref = f32[8,16,2560]{2,1,0:T(8,128)} fusion(f32[1,2,64,2560]{3,2,1,0:T(8,128)S(1)} %copy-done), kind=kLoop, calls=%fused_computation | loop fusion | bytes 2621440 | tf_op jit(solution)/shard_map/reshape | solution.py:240
  3.1 0.0 copy-start.1
  3.1 5.4 %all-to-all-start = ((f32[8,16,2560]{2,1,0:T(8,128)}), f32[8,16,2560]{2,1,0:T(8,128)S(1)}, u32[]{:S(2)}, u32[]{:S(2)}) async-start(f32[8,16,2560]{2,1,0:T(8,128)} %copy_bitcast_fusion.packed_ref), calls=%async_computation | async-start | bytes 2621440 | tf_op jit(solution)/shard_map/all_to_all | solution.py:253
  8.5 0.0 copy-done.1
  8.5 0.5 collective-permute-start
  9.0 1.6 %edge_lines.4 = f32[16,2560]{1,0:T(8,128)} custom-call(f32[8,16,2560]{2,1,0:T(8,128)} %copy_bitcast_fusion.packed_ref), custom_call_target="tpu_custom_call" | custom-call | tf_op jit(solution)/shard_map/edge_lines/pallas_call | solution.py:242
  10.6 0.7 %collective-permute-start.2 = (f32[16,2560]{1,0:T(8,128)}, f32[16,2560]{1,0:T(8,128)S(1)}, u32[]{:S(2)}, u32[]{:S(2)}) collective-permute-start(f32[16,2560]{1,0:T(8,128)} %edge_lines.4), channel_id=1, source_target_pairs={{8,4},{4,8},{9,5},{5,9},{10,6},{6,10},{11,7},{7,11},{24,20},{20,24... | collective-permute-start | bytes 491528 | tf_op jit(solution)/shard_map/ppermute | solution.py:269
  11.3 1.6 %edge_lines.5 = f32[16,2560]{1,0:T(8,128)} custom-call(f32[8,16,2560]{2,1,0:T(8,128)} %copy_bitcast_fusion.packed_ref), custom_call_target="tpu_custom_call" | custom-call | tf_op jit(solution)/shard_map/edge_lines/pallas_call | solution.py:242
  12.9 0.0 copy-start.4
  12.9 0.0 copy-start.2
  12.9 0.0 copy-start.3
  12.9 0.8 %collective-permute-start.3 = (f32[16,2560]{1,0:T(8,128)}, f32[16,2560]{1,0:T(8,128)S(1)}, u32[]{:S(2)}, u32[]{:S(2)}) collective-permute-start(f32[16,2560]{1,0:T(8,128)} %edge_lines.5), channel_id=1, source_target_pairs={{8,5},{4,9},{9,4},{5,8},{10,7},{6,11},{11,6},{7,10},{24,21},{20,25... | collective-permute-start | bytes 491528 | tf_op jit(solution)/shard_map/ppermute | solution.py:269
  13.7 1.6 %edge_lines.6 = f32[16,2560]{1,0:T(8,128)} custom-call(f32[8,16,2560]{2,1,0:T(8,128)} %copy_bitcast_fusion.packed_ref), custom_call_target="tpu_custom_call" | custom-call | tf_op jit(solution)/shard_map/edge_lines/pallas_call | solution.py:242
  15.3 0.7 %collective-permute-start.4 = (f32[16,2560]{1,0:T(8,128)}, f32[16,2560]{1,0:T(8,128)S(1)}, u32[]{:S(2)}, u32[]{:S(2)}) collective-permute-start(f32[16,2560]{1,0:T(8,128)} %edge_lines.6), channel_id=1, source_target_pairs={{8,6},{4,10},{9,7},{5,11},{10,4},{6,8},{11,5},{7,9},{24,22},{20,26... | collective-permute-start | bytes 491528 | tf_op jit(solution)/shard_map/ppermute | solution.py:269
  16.0 1.6 %edge_lines.7 = f32[16,2560]{1,0:T(8,128)} custom-call(f32[8,16,2560]{2,1,0:T(8,128)} %copy_bitcast_fusion.packed_ref), custom_call_target="tpu_custom_call" | custom-call | tf_op jit(solution)/shard_map/edge_lines/pallas_call | solution.py:242
  17.6 0.7 %collective-permute-start.5 = (f32[16,2560]{1,0:T(8,128)}, f32[16,2560]{1,0:T(8,128)S(1)}, u32[]{:S(2)}, u32[]{:S(2)}) collective-permute-start(f32[16,2560]{1,0:T(8,128)} %edge_lines.7), channel_id=1, source_target_pairs={{8,7},{4,11},{9,6},{5,10},{10,5},{6,9},{11,4},{7,8},{24,23},{20,27... | collective-permute-start | bytes 491528 | tf_op jit(solution)/shard_map/ppermute | solution.py:269
  18.3 0.0 copy-done.4
  18.3 0.1 dynamic_slice.7
  18.4 0.1 dynamic_slice.6
  18.5 0.0 copy-done.2
  18.5 0.2 convert_reduce_fusion
  18.7 0.0 copy-done.3
  18.7 0.1 maximum_multiply_fusion
  18.8 0.0 collective-permute-done
  18.8 0.7 %collective-permute-start.1 = (f32[8,2560]{1,0:T(8,128)S(1)}, f32[8,2560]{1,0:T(8,128)S(1)}, u32[]{:S(2)}, u32[]{:S(2)}) collective-permute-start(f32[8,2560]{1,0:T(8,128)S(1)} %maximum_select_fusion), channel_id=1, source_target_pairs={{0,0},{1,8},{2,1},{3,9},{4,2},{5,10},{6,3},{7,11},{8,4},{9,12},{10... | collective-permute-start | bytes 245768 | tf_op jit(solution)/shard_map/ppermute | solution.py:279
  19.5 0.1 pad_add_fusion.place_ref
  19.6 0.0 collective-permute-done.1.phase_ref
  19.6 0.0 collective-permute-done.2
  19.6 0.0 collective-permute-done.3
  19.6 0.0 collective-permute-done.4
  19.6 0.0 collective-permute-done.5
  19.6 6.2 %all-to-all-done = f32[8,16,2560]{2,1,0:T(8,128)S(1)} async-done(((f32[8,16,2560]{2,1,0:T(8,128)}), f32[8,16,2560]{2,1,0:T(8,128)S(1)}, u32[]{:S(2)}, u32[]{:S(2)}) %all-to-all-start) | async-done | bytes 1310752 | tf_op jit(solution)/shard_map/all_to_all | solution.py:253
  25.8 0.1 broadcast_in_dim.16.factor_ref
  25.9 3.8 %pair_products.1 = f32[384,128]{1,0:T(8,128)S(1)} custom-call(s32[66]{0:T(128)S(1)} %pad_add_fusion.place_ref, f32[16,128]{1,0:T(8,128)S(1)} %broadcast_in_dim.16.factor_ref, f32[8,2560]{1,0:T(8,128)S(1)} %collective-permute-done.1.phase_ref, f32[2560,128]{1,0:T(8,128)S(1)} %bitcast.52, f32[320,128]{1,0:T(8,128)S(1)} %bitcast.55, f32[320,128]{1,0:T(8,128)S(1)} %bitcast.56, ...), custom_call_target="tpu_custom_call" | custom-call | tf_op jit(solution)/shard_map/pair_products/pallas_call | solution.py:297
  29.7 23.6 %all_to_all.10 = f32[16,24,128]{2,1,0:T(8,128)S(1)} all-to-all(f32[16,24,128]{2,1,0:T(8,128)S(1)} %bitcast.53), channel_id=1, replica_groups=mesh['groups'=2,'date'=16] {'date'}, dimensions={0} | all-to-all | bytes 393216 | tf_op jit(solution)/shard_map/all_to_all | solution.py:317
  53.3 0.7 %collect_slots.1 = (f32[4,2,16,128]{3,2,1,0:T(8,128)}, f32[4,16,128]{2,1,0:T(8,128)}) custom-call(f32[384,128]{1,0:T(8,128)S(1)} %bitcast.54), custom_call_target="tpu_custom_call" | custom-call | tf_op jit(solution)/shard_map/collect_slots/pallas_call | solution.py:325
  (3 shorter events, 0.0 us)
Async XLA Ops:
  0.6 1.3 %copy-start = (f32[1,2,64,2560]{3,2,1,0:T(8,128)S(1)}, f32[1,2,64,2560]{3,2,1,0:T(8,128)}, u32[]{:S(2)}) copy-start(f32[1,2,64,2560]{3,2,1,0:T(8,128)} %param.5) | copy-start | bytes 3932164
  3.1 5.4 %copy-start.1 = (f32[4,2560]{1,0:T(4,128)S(1)}, f32[4,2560]{1,0:T(4,128)}, u32[]{:S(2)}) copy-start(f32[4,2560]{1,0:T(4,128)} %param.6) | copy-start | bytes 122884
  3.1 22.7 %all-to-all-start = ((f32[8,16,2560]{2,1,0:T(8,128)}), f32[8,16,2560]{2,1,0:T(8,128)S(1)}, u32[]{:S(2)}, u32[]{:S(2)}) async-start(f32[8,16,2560]{2,1,0:T(8,128)} %copy_bitcast_fusion.packed_ref), calls=%async_computation | async-start | bytes 2621440 | tf_op jit(solution)/shard_map/all_to_all | solution.py:253
  8.5 10.3 %collective-permute-start = (f32[4,2560]{1,0:T(4,128)S(1)}, f32[4,2560]{1,0:T(4,128)S(1)}, u32[]{:S(2)}, u32[]{:S(2)}) collective-permute-start(f32[4,2560]{1,0:T(4,128)S(1)} %copy-done.1), channel_id=1, source_target_pairs={{0,1},{1,0},{2,3},{3,2},{4,5},{5,4},{6,7},{7,6},{8,9},{9,8},{10,11... | collective-permute-start | bytes 122888 | tf_op jit(solution)/shard_map/ppermute | solution.py:237
  10.6 9.0 %collective-permute-start.2 = (f32[16,2560]{1,0:T(8,128)}, f32[16,2560]{1,0:T(8,128)S(1)}, u32[]{:S(2)}, u32[]{:S(2)}) collective-permute-start(f32[16,2560]{1,0:T(8,128)} %edge_lines.4), channel_id=1, source_target_pairs={{8,4},{4,8},{9,5},{5,9},{10,6},{6,10},{11,7},{7,11},{24,20},{20,24... | collective-permute-start | bytes 491528 | tf_op jit(solution)/shard_map/ppermute | solution.py:269
  12.9 5.4 %copy-start.4 = (f32[16]{0:T(128)S(1)}, f32[16]{0:T(128)}, u32[]{:S(2)}) copy-start(f32[16]{0:T(128)} %param.7) | copy-start | bytes 196
  12.9 5.6 %copy-start.2 = (s32[32,1]{0,1:T(1,128)S(1)}, s32[32,1]{0,1:T(1,128)}, u32[]{:S(2)}) copy-start(s32[32,1]{0,1:T(1,128)} %param.9) | copy-start | bytes 388
  12.9 5.8 %copy-start.3 = (s32[32,2]{0,1:T(2,128)S(1)}, s32[32,2]{0,1:T(2,128)}, u32[]{:S(2)}) copy-start(s32[32,2]{0,1:T(2,128)} %param.8) | copy-start | bytes 772
  12.9 6.7 %collective-permute-start.3 = (f32[16,2560]{1,0:T(8,128)}, f32[16,2560]{1,0:T(8,128)S(1)}, u32[]{:S(2)}, u32[]{:S(2)}) collective-permute-start(f32[16,2560]{1,0:T(8,128)} %edge_lines.5), channel_id=1, source_target_pairs={{8,5},{4,9},{9,4},{5,8},{10,7},{6,11},{11,6},{7,10},{24,21},{20,25... | collective-permute-start | bytes 491528 | tf_op jit(solution)/shard_map/ppermute | solution.py:269
  15.3 4.2 %collective-permute-start.4 = (f32[16,2560]{1,0:T(8,128)}, f32[16,2560]{1,0:T(8,128)S(1)}, u32[]{:S(2)}, u32[]{:S(2)}) collective-permute-start(f32[16,2560]{1,0:T(8,128)} %edge_lines.6), channel_id=1, source_target_pairs={{8,6},{4,10},{9,7},{5,11},{10,4},{6,8},{11,5},{7,9},{24,22},{20,26... | collective-permute-start | bytes 491528 | tf_op jit(solution)/shard_map/ppermute | solution.py:269
  17.6 2.0 %collective-permute-start.5 = (f32[16,2560]{1,0:T(8,128)}, f32[16,2560]{1,0:T(8,128)S(1)}, u32[]{:S(2)}, u32[]{:S(2)}) collective-permute-start(f32[16,2560]{1,0:T(8,128)} %edge_lines.7), channel_id=1, source_target_pairs={{8,7},{4,11},{9,6},{5,10},{10,5},{6,9},{11,4},{7,8},{24,23},{20,27... | collective-permute-start | bytes 491528 | tf_op jit(solution)/shard_map/ppermute | solution.py:269
  18.8 0.8 %collective-permute-start.1 = (f32[8,2560]{1,0:T(8,128)S(1)}, f32[8,2560]{1,0:T(8,128)S(1)}, u32[]{:S(2)}, u32[]{:S(2)}) collective-permute-start(f32[8,2560]{1,0:T(8,128)S(1)} %maximum_select_fusion), channel_id=1, source_target_pairs={{0,0},{1,8},{2,1},{3,9},{4,2},{5,10},{6,3},{7,11},{8,4},{9,12},{10... | collective-permute-start | bytes 245768 | tf_op jit(solution)/shard_map/ppermute | solution.py:279

commit v6 on v3

--- a/solution.py
+++ b/solution.py
@@ -100,6 +100,7 @@
         return real * cosine - imag * sine_part, real * sine_part + imag * cosine
 
     first_row = row_index < BAND
+    wide = jnp.broadcast_to(factor_ref[...], (half + SUB, LANES))
     to_even = SUB // 2 * side
     to_odd = SUB // 2 - to_even
     edge_kind = 1 + 2 * BAND
@@ -123,7 +124,7 @@
                 phases = [phase_ref[line : line + 1, column] for line in (even, even + 1)]
                 span = slice(even * BAND, even * BAND + SUB)
                 edge = turned(
-                    factor_ref[tiles * SUB :, :] * jnp.where(first_row, *phases),
+                    wide[tiles * SUB :, :] * jnp.where(first_row, *phases),
                     raw_ref[0, span, :],
                     raw_ref[1, span, :],
                 )
@@ -136,7 +137,7 @@
                     for tile in range(tiles):
                         start = tile * SUB * per_date + line_at + line
                         real, imag = turned(
-                            factor_ref[tile * SUB : (tile + 1) * SUB, :]
+                            wide[tile * SUB : (tile + 1) * SUB, :]
                             * phases[line - even],
                             own_ref[pl.ds(start, SUB, stride=per_date), :],
                             own_ref[pl.ds(start + per_part, SUB, stride=per_date), :],
@@ -162,7 +163,7 @@
     def sum_row(kind, b, tile):
         return (kind * tiles * ROW_SETS + b * (1 if kind == edge_kind else tiles) + tile) * SUB
 
-    lax.fori_loop(0, blocks, block, 0, unroll=4 if tiles == 1 else 1)
+    lax.fori_loop(0, blocks, block, 0, unroll=10 if tiles == 1 else 1)
 
     box = box_ref[...]
     looked = None
@@ -289,7 +290,7 @@
         baseline, jnp.where(low, half, half - BAND), BAND
     )
     factors = 0.5 * jnp.concatenate([own_factors, edge_factors, edge_factors])
-    factors = jnp.broadcast_to(factors[:, None], (half + SUB, LANES))
+    factors = factors[:, None]
     sums = ((1 + 2 * BAND) * tiles + 1) * ROW_SETS * SUB
     slot_rows = devices * CAP * SLOT_ROWS
     owners = pair_owner[:, 0]

time: 51.4 us -> 51.4 us (level)
  no operation moved by 1% of the time
where the time goes in v6:
time: 51.4 us; the launch traced here: 51 us
  blocking collectives  20.7 us (40%)
  waiting for transfers between devices  10.5 us (20%)
  starting transfers between devices  9.29 us (18%)
  Pallas kernels  6.53 us (13%)
  local copies, waits for them, and re-layouts  2.75 us (5%)
  between operations  0.84 us (2%)
    all_to_all x1, blocking collectives, body(): lax.all_to_all(buffer.reshape(devices, CAP * SLOT_ROWS, LANES), 'date', s...  20.7 us
    all_to_all x1, waiting for transfers between devices, body(): lax.all_to_all(packed, 'date', split_axis=0, concat_axis=0, tiled=True, a...  10.5 us
    all_to_all x1, starting transfers between devices, body(): lax.all_to_all(packed, 'date', split_axis=0, concat_axis=0, tiled=True, a...  5.39 us
    pallas_call x1, Pallas kernels, body(): pl.pallas_call(functools.partial(pair_kernel, half, blocks, pairs), out_s...  3.85 us
    ppermute x4, starting transfers between devices, body(): got = lax.ppermute(edges[BAND * g + i], 'date', steps)  2.68 us
    pallas_call x1, Pallas kernels, body(): pl.pallas_call(functools.partial(edge_kernel, half), out_shape=[jax.Shape...  2.01 us
    unnamed x10, local copies, waits for them, and re-layouts  1.34 us
    reshape x1, local copies, waits for them, and re-layouts, body(): packed = packed.reshape(half, 2 * SUB, columns)  1.17 us
  transfers between devices with their start and end apart: 7, of which 1 were waited for; matrix products, arithmetic and copies ran while one was open for 1% of the time, Pallas kernels for 4%

profile of v6, /device:TPU:0, one launch (start us, length us, event | category | flops | bytes accessed | tf_op | source)
XLA Modules:
  0.0 51.0 jit_solution(3744453482870037516)
XLA Ops:
  0.6 0.0 copy-start
  0.6 1.3 %copy-done = f32[1,2,64,2560]{3,2,1,0:T(8,128)S(1)} copy-done((f32[1,2,64,2560]{3,2,1,0:T(8,128)S(1)}, f32[1,2,64,2560]{3,2,1,0:T(8,128)}, u32[]{:S(2)}) %copy-start) | copy-done | bytes 1310744
  2.0 1.2 %copy_bitcast_fusion.packed_ref = f32[8,16,2560]{2,1,0:T(8,128)} fusion(f32[1,2,64,2560]{3,2,1,0:T(8,128)S(1)} %copy-done), kind=kLoop, calls=%fused_computation | loop fusion | bytes 2621440 | tf_op jit(solution)/shard_map/reshape | solution.py:249
  3.1 0.0 copy-start.1
  3.1 5.4 %all-to-all-start = ((f32[8,16,2560]{2,1,0:T(8,128)}), f32[8,16,2560]{2,1,0:T(8,128)S(1)}, u32[]{:S(2)}, u32[]{:S(2)}) async-start(f32[8,16,2560]{2,1,0:T(8,128)} %copy_bitcast_fusion.packed_ref), calls=%async_computation | async-start | bytes 2621440 | tf_op jit(solution)/shard_map/all_to_all | solution.py:259
  8.5 0.0 copy-done.1
  8.5 0.0 copy-start.4
  8.5 0.0 copy-start.2
  8.5 0.0 copy-start.3
  8.6 0.6 %collective-permute-start = (f32[4,2560]{1,0:T(4,128)S(1)}, f32[4,2560]{1,0:T(4,128)S(1)}, u32[]{:S(2)}, u32[]{:S(2)}) collective-permute-start(f32[4,2560]{1,0:T(4,128)S(1)} %copy-done.1), channel_id=1, source_target_pairs={{0,1},{1,0},{2,3},{3,2},{4,5},{5,4},{6,7},{7,6},{8,9},{9,8},{10,11... | collective-permute-start | bytes 122888 | tf_op jit(solution)/shard_map/ppermute | solution.py:246
  9.1 2.0 %edge_lines.1 = (f32[16,2560]{1,0:T(8,128)}, f32[16,2560]{1,0:T(8,128)}, f32[16,2560]{1,0:T(8,128)}, f32[16,2560]{1,0:T(8,128)}) custom-call(f32[8,16,2560]{2,1,0:T(8,128)} %copy_bitcast_fusion.packed_ref), custom_call_target="tpu_custom_call" | custom-call | tf_op jit(solution)/shard_map/edge_lines/pallas_call | solution.py:250
  11.1 0.7 %collective-permute-start.2 = (f32[16,2560]{1,0:T(8,128)}, f32[16,2560]{1,0:T(8,128)S(1)}, u32[]{:S(2)}, u32[]{:S(2)}) collective-permute-start(f32[16,2560]{1,0:T(8,128)} %get-tuple-element.6), channel_id=1, source_target_pairs={{8,4},{4,8},{9,5},{5,9},{10,6},{6,10},{11,7},{7,11},{24,20},{20,24... | collective-permute-start | bytes 491528 | tf_op jit(solution)/shard_map/ppermute | solution.py:275
  11.8 0.7 %collective-permute-start.3 = (f32[16,2560]{1,0:T(8,128)}, f32[16,2560]{1,0:T(8,128)S(1)}, u32[]{:S(2)}, u32[]{:S(2)}) collective-permute-start(f32[16,2560]{1,0:T(8,128)} %get-tuple-element.7), channel_id=1, source_target_pairs={{8,5},{4,9},{9,4},{5,8},{10,7},{6,11},{11,6},{7,10},{24,21},{20,25... | collective-permute-start | bytes 491528 | tf_op jit(solution)/shard_map/ppermute | solution.py:275
  12.5 0.7 %collective-permute-start.4 = (f32[16,2560]{1,0:T(8,128)}, f32[16,2560]{1,0:T(8,128)S(1)}, u32[]{:S(2)}, u32[]{:S(2)}) collective-permute-start(f32[16,2560]{1,0:T(8,128)} %get-tuple-element.8), channel_id=1, source_target_pairs={{8,6},{4,10},{9,7},{5,11},{10,4},{6,8},{11,5},{7,9},{24,22},{20,26... | collective-permute-start | bytes 491528 | tf_op jit(solution)/shard_map/ppermute | solution.py:275
  13.2 0.7 %collective-permute-start.5 = (f32[16,2560]{1,0:T(8,128)}, f32[16,2560]{1,0:T(8,128)S(1)}, u32[]{:S(2)}, u32[]{:S(2)}) collective-permute-start(f32[16,2560]{1,0:T(8,128)} %get-tuple-element.9), channel_id=1, source_target_pairs={{8,7},{4,11},{9,6},{5,10},{10,5},{6,9},{11,4},{7,8},{24,23},{20,27... | collective-permute-start | bytes 491528 | tf_op jit(solution)/shard_map/ppermute | solution.py:275
  13.9 0.0 copy-done.4
  13.9 0.1 dynamic-slice_bitcast_fusion
  14.0 0.1 dynamic-slice_bitcast_fusion.1
  14.0 0.1 pad_maximum_fusion
  14.1 0.1 copy.15
  14.2 0.0 copy-done.2
  14.2 0.2 convert_reduce_fusion
  14.4 0.0 copy-done.3
  14.4 0.0 collective-permute-done
  14.5 0.7 %collective-permute-start.1 = (f32[8,2560]{1,0:T(8,128)S(1)}, f32[8,2560]{1,0:T(8,128)S(1)}, u32[]{:S(2)}, u32[]{:S(2)}) collective-permute-start(f32[8,2560]{1,0:T(8,128)S(1)} %maximum_select_fusion), channel_id=1, source_target_pairs={{0,0},{1,8},{2,1},{3,9},{4,2},{5,10},{6,3},{7,11},{8,4},{9,12},{10... | collective-permute-start | bytes 245768 | tf_op jit(solution)/shard_map/ppermute | solution.py:285
  15.2 0.1 pad_add_fusion.place_ref
  15.2 0.0 collective-permute-done.1.phase_ref
  15.3 0.0 collective-permute-done.2
  15.3 0.0 collective-permute-done.3
  15.3 0.0 collective-permute-done.4
  15.3 0.0 collective-permute-done.5
  15.3 10.5 %all-to-all-done = f32[8,16,2560]{2,1,0:T(8,128)S(1)} async-done(((f32[8,16,2560]{2,1,0:T(8,128)}), f32[8,16,2560]{2,1,0:T(8,128)S(1)}, u32[]{:S(2)}, u32[]{:S(2)}) %all-to-all-start) | async-done | bytes 1310752 | tf_op jit(solution)/shard_map/all_to_all | solution.py:259
  25.8 3.8 %pair_products.1 = f32[384,128]{1,0:T(8,128)S(1)} custom-call(s32[66]{0:T(128)S(1)} %pad_add_fusion.place_ref, f32[16,1]{1,0:T(8,128)S(1)} %broadcast_multiply_fusion.factor_ref, f32[8,2560]{1,0:T(8,128)S(1)} %collective-permute-done.1.phase_ref, f32[2560,128]{1,0:T(8,128)S(1)} %bitcast.56, f32[320,128]{1,0:T(8,128)S(1)} %bitcast.59, ...), custom_call_target="tpu_custom_call" | custom-call | tf_op jit(solution)/shard_map/pair_products/pallas_call | solution.py:303
  29.6 20.7 %all_to_all.10 = f32[16,24,128]{2,1,0:T(8,128)S(1)} all-to-all(f32[16,24,128]{2,1,0:T(8,128)S(1)} %bitcast.57), channel_id=1, replica_groups=mesh['groups'=2,'date'=16] {'date'}, dimensions={0} | all-to-all | bytes 393216 | tf_op jit(solution)/shard_map/all_to_all | solution.py:323
  50.3 0.7 %collect_slots.1 = (f32[4,2,16,128]{3,2,1,0:T(8,128)}, f32[4,16,128]{2,1,0:T(8,128)}) custom-call(f32[384,128]{1,0:T(8,128)S(1)} %bitcast.58), custom_call_target="tpu_custom_call" | custom-call | tf_op jit(solution)/shard_map/collect_slots/pallas_call | solution.py:331
  (4 shorter events, 0.1 us)
Async XLA Ops:
  0.6 1.3 %copy-start = (f32[1,2,64,2560]{3,2,1,0:T(8,128)S(1)}, f32[1,2,64,2560]{3,2,1,0:T(8,128)}, u32[]{:S(2)}) copy-start(f32[1,2,64,2560]{3,2,1,0:T(8,128)} %param.5) | copy-start | bytes 3932164
  3.1 5.4 %copy-start.1 = (f32[4,2560]{1,0:T(4,128)S(1)}, f32[4,2560]{1,0:T(4,128)}, u32[]{:S(2)}) copy-start(f32[4,2560]{1,0:T(4,128)} %param.6) | copy-start | bytes 122884
  3.1 22.7 %all-to-all-start = ((f32[8,16,2560]{2,1,0:T(8,128)}), f32[8,16,2560]{2,1,0:T(8,128)S(1)}, u32[]{:S(2)}, u32[]{:S(2)}) async-start(f32[8,16,2560]{2,1,0:T(8,128)} %copy_bitcast_fusion.packed_ref), calls=%async_computation | async-start | bytes 2621440 | tf_op jit(solution)/shard_map/all_to_all | solution.py:259
  8.5 5.4 %copy-start.4 = (f32[16]{0:T(128)S(1)}, f32[16]{0:T(128)}, u32[]{:S(2)}) copy-start(f32[16]{0:T(128)} %param.7) | copy-start | bytes 196
  8.5 5.7 %copy-start.2 = (s32[32,1]{0,1:T(1,128)S(1)}, s32[32,1]{0,1:T(1,128)}, u32[]{:S(2)}) copy-start(s32[32,1]{0,1:T(1,128)} %param.9) | copy-start | bytes 388
  8.5 5.9 %copy-start.3 = (s32[32,2]{0,1:T(2,128)S(1)}, s32[32,2]{0,1:T(2,128)}, u32[]{:S(2)}) copy-start(s32[32,2]{0,1:T(2,128)} %param.8) | copy-start | bytes 772
  8.6 5.9 %collective-permute-start = (f32[4,2560]{1,0:T(4,128)S(1)}, f32[4,2560]{1,0:T(4,128)S(1)}, u32[]{:S(2)}, u32[]{:S(2)}) collective-permute-start(f32[4,2560]{1,0:T(4,128)S(1)} %copy-done.1), channel_id=1, source_target_pairs={{0,1},{1,0},{2,3},{3,2},{4,5},{5,4},{6,7},{7,6},{8,9},{9,8},{10,11... | collective-permute-start | bytes 122888 | tf_op jit(solution)/shard_map/ppermute | solution.py:246
  11.1 4.1 %collective-permute-start.2 = (f32[16,2560]{1,0:T(8,128)}, f32[16,2560]{1,0:T(8,128)S(1)}, u32[]{:S(2)}, u32[]{:S(2)}) collective-permute-start(f32[16,2560]{1,0:T(8,128)} %get-tuple-element.6), channel_id=1, source_target_pairs={{8,4},{4,8},{9,5},{5,9},{10,6},{6,10},{11,7},{7,11},{24,20},{20,24... | collective-permute-start | bytes 491528 | tf_op jit(solution)/shard_map/ppermute | solution.py:275
  11.8 3.4 %collective-permute-start.3 = (f32[16,2560]{1,0:T(8,128)}, f32[16,2560]{1,0:T(8,128)S(1)}, u32[]{:S(2)}, u32[]{:S(2)}) collective-permute-start(f32[16,2560]{1,0:T(8,128)} %get-tuple-element.7), channel_id=1, source_target_pairs={{8,5},{4,9},{9,4},{5,8},{10,7},{6,11},{11,6},{7,10},{24,21},{20,25... | collective-permute-start | bytes 491528 | tf_op jit(solution)/shard_map/ppermute | solution.py:275
  12.5 2.8 %collective-permute-start.4 = (f32[16,2560]{1,0:T(8,128)}, f32[16,2560]{1,0:T(8,128)S(1)}, u32[]{:S(2)}, u32[]{:S(2)}) collective-permute-start(f32[16,2560]{1,0:T(8,128)} %get-tuple-element.8), channel_id=1, source_target_pairs={{8,6},{4,10},{9,7},{5,11},{10,4},{6,8},{11,5},{7,9},{24,22},{20,26... | collective-permute-start | bytes 491528 | tf_op jit(solution)/shard_map/ppermute | solution.py:275
  13.2 2.1 %collective-permute-start.5 = (f32[16,2560]{1,0:T(8,128)}, f32[16,2560]{1,0:T(8,128)S(1)}, u32[]{:S(2)}, u32[]{:S(2)}) collective-permute-start(f32[16,2560]{1,0:T(8,128)} %get-tuple-element.9), channel_id=1, source_target_pairs={{8,7},{4,11},{9,6},{5,10},{10,5},{6,9},{11,4},{7,8},{24,23},{20,27... | collective-permute-start | bytes 491528 | tf_op jit(solution)/shard_map/ppermute | solution.py:275
  14.5 0.8 %collective-permute-start.1 = (f32[8,2560]{1,0:T(8,128)S(1)}, f32[8,2560]{1,0:T(8,128)S(1)}, u32[]{:S(2)}, u32[]{:S(2)}) collective-permute-start(f32[8,2560]{1,0:T(8,128)S(1)} %maximum_select_fusion), channel_id=1, source_target_pairs={{0,0},{1,8},{2,1},{3,9},{4,2},{5,10},{6,3},{7,11},{8,4},{9,12},{10... | collective-permute-start | bytes 245768 | tf_op jit(solution)/shard_map/ppermute | solution.py:285
